TPU v7x, 512 devices: a whole 4x4x16 slice. The times are simulated.
512 devices in a mesh: px: 32 (over z, y_hi), py: 16 (over x, y_lo, core).
Axes of the slice: x: 4, y: 4 (y_hi: 2, y_lo: 2; y = y_hi * 2 + y_lo), z: 16, core: 2. Of those that a mesh axis runs over, the one named last changes fastest.
Arguments:
- residual: float32 [512, 1792, 128], P('px', 'py'), may hold values from -6 to 6
- basis: float32 [4, 512, 1792], P(None, 'px', 'py'), may hold values from -0.6 to 0.6
- inv_blocks: bfloat16 [32, 16, 32, 3, 128, 128], P('px', 'py'), may hold values from -0.3125 to 0.3125
- pattern: int32 [32, 16, 32, 3], P('px', 'py'), may hold values from 0 to 31
- coarse_map: int32 [32, 16, 4], replicated, may hold values from 0 to 2047
- coarse_inv: float32 [2048, 2048], P(('px', 'py')), may hold values from -0.125 to 0.125
Outputs:
- preconditioned: float32 [512, 1792, 128], P('px', 'py')
All inputs are finite; a program needn't handle non-finite values.
Results may differ from a plain program's by a relative error of at most 0.0022.
Values may be sent and summed in bfloat16 or wider, within the bound.
No kernel may reach another device: no remote copies, remote signals or barrier semaphores. Data moves between devices by JAX's collectives and lax.ppermute only.
A program may use at most 64 MiB of HBM per device.

v0:
```python
import jax
import jax.numpy as jnp
from jax import lax
from jax.sharding import PartitionSpec as P

W = 8
K = 3


def with_halo(cells, sides, width):
    for axis, dim in sides:
        count = lax.axis_size(axis)
        ends = count - 1
        head = lax.slice_in_dim(cells, 0, width, axis=dim)
        tail = lax.slice_in_dim(cells, cells.shape[dim] - width, cells.shape[dim], axis=dim)
        cells = jnp.concatenate(
            [
                lax.ppermute(tail, axis, [(i, (i + 1) % count) for i in range(ends)]),
                cells,
                lax.ppermute(head, axis, [((i + 1) % count, i) for i in range(ends)]),
            ],
            axis=dim,
        )
    return cells


def body(residual, basis, inv_blocks, pattern, coarse_map, coarse_inv):
    own_x = residual.shape[0]
    own_y = residual.shape[1]
    vectors = residual.shape[2]
    rounded = residual.astype(jnp.bfloat16)
    ext = with_halo(rounded, (("px", 0), ("py", 1)), W)
    block_rows = ext.shape[0]
    picked = jnp.take(ext, pattern[0, 0].reshape(-1), axis=0).reshape(
        block_rows, K, ext.shape[1], vectors
    )
    solved = jnp.einsum(
        "ikyz,ikzr->iyr", inv_blocks[0, 0], picked, preferred_element_type=jnp.float32
    )
    local_part = solved[W : W + own_x, W : W + own_y]
    contrib = jnp.einsum("lxy,xyr->lr", basis, residual, precision=lax.Precision.HIGHEST)
    total_coarse = coarse_inv.shape[1]
    own_ids = coarse_map[lax.axis_index("px"), lax.axis_index("py")]
    selector = (own_ids[:, None] == jnp.arange(total_coarse, dtype=jnp.int32)[None, :]).astype(
        jnp.float32
    )
    spread_res = jnp.dot(selector.T, contrib, precision=lax.Precision.HIGHEST)
    coarse_res = lax.psum(spread_res, ("px", "py"))
    sol_rows = jnp.dot(coarse_inv, coarse_res, precision=lax.Precision.HIGHEST)
    coarse_sol = lax.all_gather(sol_rows, ("px", "py"), axis=0, tiled=True)
    local_sol = jnp.dot(selector, coarse_sol, precision=lax.Precision.HIGHEST)
    correction = jnp.einsum("lxy,lr->xyr", basis, local_sol, precision=lax.Precision.HIGHEST)
    return local_part + correction


def solution(mesh):
    return jax.shard_map(
        body,
        mesh=mesh,
        in_specs=(
            P("px", "py", None),
            P(None, "px", "py"),
            P("px", "py", None, None, None, None),
            P("px", "py", None, None),
            P(),
            P(("px", "py"), None),
        ),
        out_specs=P("px", "py", None),
        check_vma=False,
    )
```

profile of v0, /device:TPU:1, one launch (start us, length us, event | category | flops | bytes accessed | tf_op | source)
XLA Modules:
  0.0 1246.8 jit_solution(9190478112845996960)
XLA Ops:
  6.5 0.0 copy-start
  6.5 0.0 all-reduce.2.cloned.1.call-start
  6.5 0.0 copy-start.3
  6.5 2.2 convolution_bitcast_fusion.3
  8.8 0.9 dynamic-slice_reduce_fusion
  9.6 2.1 fusion.11
  11.7 0.0 all-reduce.2.cloned.1.call-update
  11.8 0.0 all-gather.3.cloned.1.call-start
  11.8 473.5 %all-reduce.2.cloned.1.call-done = f32[2048,128]{1,0:T(8,128)} async-done(((f32[2048,128]{1,0:T(8,128)}), f32[2048,128]{1,0:T(8,128)}) %all-reduce.2.cloned.1.call-update) | async-done | bytes 1048592 | tf_op jit(solution)/shard_map/psum | solution.py:48
  485.3 2.5 convolution_bitcast_fusion.2
  487.8 0.0 all-gather.3.cloned.1.call-update
  487.8 1.2 convert_element_type.4
  489.1 0.0 copy-start.1
  489.1 0.8 copy-done.1
  489.8 0.8 fusion.18
  490.7 4.4 collective-permute-start
  495.1 1.3 collective-permute-start.1
  496.4 0.0 copy-done.3
  496.4 0.1 copy.14
  496.5 0.1 copy.13
  496.6 0.1 reshape_squeeze.6
  496.7 8.4 collective-permute-done
  505.1 0.4 collective-permute-done.1
  505.5 0.8 pad_maximum_fusion.3
  506.3 3.5 collective-permute-start.2
  509.8 1.9 collective-permute-start.3
  511.8 0.0 collective-permute-done.2
  511.8 3.6 collective-permute-done.3
  515.4 2.3 pad_maximum_fusion
  517.7 3.9 gather_fusion
  521.6 0.0 copy-done
  521.6 0.0 copy-start.2
  521.6 4.3 fusion.4
  525.9 708.7 %all-gather.3.cloned.1.call-done = f32[512,4,128]{2,1,0:T(4,128)} async-done(((f32[1,4,128]{2,1,0:T(4,128)}), f32[512,4,128]{2,1,0:T(4,128)}) %all-gather.3.cloned.1.call-update) | async-done | bytes 1048592 | tf_op jit(solution)/shard_map/all_gather | solution.py:50
  1234.6 1.7 convolution_bitcast_fusion.1
  1236.2 0.0 copy-done.2
  1236.2 3.7 fusion.10
  (3 shorter events, 0.0 us)
Async XLA Ops:
  6.5 515.0 %copy-start = (bf16[1,1,32,3,128,128]{5,4,3,2,1,0:T(8,128)(2,1)S(1)}, bf16[1,1,32,3,128,128]{5,4,3,2,1,0:T(8,128)(2,1)}, u32[]{:S(2)}) copy-start(bf16[1,1,32,3,128,128]{5,4,3,2,1,0:T(8,128)(2,1)} %param.8) | copy-start | bytes 9437188
  6.5 478.8 %all-reduce.2.cloned.1.call-start = ((), (), s32[]{:S(2)}) async-start(), calls=%async_computation | async-start | bytes 2097152 | tf_op jit(solution)/shard_map/psum | solution.py:48
  6.5 489.9 %copy-start.3 = (s32[1,1,32,3]{2,1,3,0:T(1,128)S(1)}, s32[1,1,32,3]{2,1,3,0:T(1,128)}, u32[]{:S(2)}) copy-start(s32[1,1,32,3]{2,1,3,0:T(1,128)} %param.9) | copy-start | bytes 1156
  11.8 1222.8 %all-gather.3.cloned.1.call-start = ((), (), s32[]{:S(2)}) async-start(), calls=%async_computation.1 | async-start | bytes 1050624 | tf_op jit(solution)/shard_map/all_gather | solution.py:50
  489.1 0.8 copy-start.1
  490.7 14.5 %collective-permute-start = (bf16[8,112,128]{2,1,0:T(8,128)(2,1)}, bf16[8,112,128]{2,1,0:T(8,128)(2,1)S(1)}, u32[]{:S(2)}, u32[]{:S(2)}) collective-permute-start(bf16[8,112,128]{2,1,0:T(8,128)(2,1)} %get-tuple-element.7), channel_id=1, source_target_pairs={{0,16},{16,32},{32,48},{48,64},{64,80},{80,96},{96,112},{112,128},... | collective-permute-start | bytes 688136 | tf_op jit(solution)/shard_map/ppermute | solution.py:18
  495.1 10.4 collective-permute-start.1
  506.3 5.4 collective-permute-start.2
  509.8 5.6 collective-permute-start.3
  521.6 714.7 %copy-start.2 = (f32[4,16,112]{2,1,0:T(8,128)S(1)}, f32[4,16,112]{2,1,0:T(8,128)}, u32[]{:S(2)}) copy-start(f32[4,16,112]{2,1,0:T(8,128)} %param.7) | copy-start | bytes 86020
Sparse Core Ops, SparseCore 0:
  12.8 472.4 all-reduce.1
  488.0 746.5 all-gather.2
where the time goes:
time: 1250 us
  waiting for transfers between devices  1190 us (95%)
  matrix products  16.5 us (1%)
  between operations  13.5 us (1%)
    all_gather x1, waiting for transfers between devices, body(): coarse_sol = lax.all_gather(sol_rows, ('px', 'py'), axis=0, tiled=True)  709 us
    psum x1, waiting for transfers between devices, body(): coarse_res = lax.psum(spread_res, ('px', 'py'))  474 us
  transfers between devices with their start and end apart: 6, of which 5 were waited for; matrix products, arithmetic and copies ran while one was open for 1% of the time, Pallas kernels for 0%

commit v1 on v0

v1 whole, which is shorter than its diff:
```python
import jax
import jax.numpy as jnp
from jax import lax
from jax.sharding import Mesh, PartitionSpec as P

W = 8
K = 3
BF = jnp.bfloat16
F32 = jnp.float32
HIGH = lax.Precision.HIGHEST


def shifted(cells, axis, dim, width):
    count = lax.axis_size(axis)
    ends = count - 1
    head = lax.slice_in_dim(cells, 0, width, axis=dim)
    tail = lax.slice_in_dim(cells, cells.shape[dim] - width, cells.shape[dim], axis=dim)
    return [
        lax.ppermute(tail, axis, [(i, i + 1) for i in range(ends)]),
        cells,
        lax.ppermute(head, axis, [(i + 1, i) for i in range(ends)]),
    ]


def local_solve(rounded, inv_blocks, pattern):
    own_x, own_y, vectors = rounded.shape
    ext = jnp.concatenate(shifted(rounded, "py", 1, W), axis=1)
    ext = jnp.concatenate(shifted(ext, ("z", "h"), 0, W), axis=0)
    wanted = pattern[0, 0, W : W + own_x]
    picked = jnp.take(ext, wanted.reshape(-1), axis=0).reshape(own_x, K, ext.shape[1], vectors)
    solved = jnp.einsum(
        "ikyz,ikzr->iyr", inv_blocks[0, 0, W : W + own_x], picked, preferred_element_type=F32
    )
    return solved[:, W : W + own_y]


def body(residual, basis, inv_blocks, pattern, coarse_map, coarse_inv):
    nz = lax.axis_size("z")
    nh = lax.axis_size("h")
    ny = lax.axis_size("py")
    plane = nh * ny
    ncl, own_x, own_y = basis.shape
    vectors = residual.shape[2]
    total = coarse_inv.shape[1]
    rounded = residual.astype(BF)
    local_part = local_solve(rounded, inv_blocks, pattern)

    ids = coarse_map.reshape(-1)
    spread = (jnp.arange(total, dtype=jnp.int32)[:, None] == ids[None, :]).astype(BF)
    ordered = jnp.dot(coarse_inv.astype(BF), spread, preferred_element_type=F32).astype(BF)
    columns = ordered.reshape(ncl, nz, plane * ncl).transpose(1, 0, 2)
    column = lax.all_to_all(columns, "z", 0, 0)

    me = lax.axis_index("h") * ny + lax.axis_index("py")
    wanted = coarse_map.reshape(nz, plane, ncl).transpose(1, 0, 2).reshape(-1)
    owner = wanted // ncl
    place = jnp.where(owner % plane == me, (owner // plane) * ncl + wanted % ncl, -1)
    pick = (place[:, None] == jnp.arange(nz * ncl)[None, :]).astype(BF)
    sent = jnp.dot(pick, column.reshape(nz * ncl, plane * ncl), preferred_element_type=F32).astype(BF)
    contrib = jnp.einsum("lxy,xyr->lr", basis, residual, precision=HIGH).astype(BF)
    sent = jnp.concatenate(
        [sent.reshape(plane, nz * ncl, plane * ncl), jnp.broadcast_to(contrib, (plane,) + contrib.shape)], axis=1
    )
    got = lax.all_to_all(sent, ("h", "py"), 0, 0)
    needed = jnp.sum(got[:, : nz * ncl].astype(F32), axis=0).astype(BF)
    every = got[:, nz * ncl :].reshape(plane * ncl, vectors)
    partial = jnp.dot(needed, every, preferred_element_type=F32)
    shares = lax.all_to_all(partial.reshape(nz, ncl, vectors), "z", 0, 0)
    local_sol = jnp.sum(shares, axis=0)
    correction = jnp.einsum("lxy,lr->xyr", basis, local_sol, precision=HIGH)
    return local_part + correction


def solution(mesh):
    count_x, count_y = mesh.devices.shape
    fine = Mesh(mesh.devices.reshape(count_x // 2, 2, count_y), ("z", "h", "py"))
    px = ("z", "h")
    return jax.shard_map(
        body,
        mesh=fine,
        in_specs=(
            P(px, "py", None),
            P(None, px, "py"),
            P(px, "py", None, None, None, None),
            P(px, "py", None, None),
            P(),
            P(("z", "h", "py"), None),
        ),
        out_specs=P(px, "py", None),
        check_vma=False,
    )
```

time: 1250 us -> 93 us (0.07)
  waiting for transfers between devices: 1190 us -> 31.8 us
  starting transfers between devices: 11.2 us -> 42.7 us
  between operations: 13.5 us -> 0.24 us
    all_gather x1 -> x0, waiting for transfers between devices: 709 us -> none  [body(): coarse_sol = lax.all_gather(sol_rows, ('px', 'py'), axis=0, tiled=True)]
    psum x1 -> x0, waiting for transfers between devices: 474 us -> none  [body(): coarse_res = lax.psum(spread_res, ('px', 'py'))]
    all_to_all x0 -> x3, starting transfers between devices: none -> 26.5 us  [the longest x1 11.4 us: body(): column = lax.all_to_all(columns, 'z', 0, 0)]
    all_to_all x0 -> x3, waiting for transfers between devices: none -> 18.5 us  [the longest x1 9.44 us: body(): column = lax.all_to_all(columns, 'z', 0, 0)]
  transfers between devices with their start and end apart: 6 -> 7, of which waited for: 5 -> 3; matrix products, arithmetic and copies ran while one was open for 1% -> 13% of each run, Pallas kernels for 0% -> 0%
where the time goes in v1:
time: 93 us; the launch traced here: 92.5 us
  starting transfers between devices  42.7 us (46%)
  waiting for transfers between devices  31.8 us (34%)
  matrix products  10.6 us (11%)
  local copies, waits for them, and re-layouts  4.67 us (5%)
  other arithmetic  2.44 us (3%)
    ppermute x2, waiting for transfers between devices, shifted(): lax.ppermute(tail, axis, [(i, i + 1) for i in range(ends)])  13.4 us
    all_to_all x1, starting transfers between devices, body(): column = lax.all_to_all(columns, 'z', 0, 0)  11.4 us
    all_to_all x1, starting transfers between devices, body(): got = lax.all_to_all(sent, ('h', 'py'), 0, 0)  10 us
    all_to_all x1, waiting for transfers between devices, body(): column = lax.all_to_all(columns, 'z', 0, 0)  9.44 us
    ppermute x2, starting transfers between devices, shifted(): lax.ppermute(tail, axis, [(i, i + 1) for i in range(ends)])  9.41 us
    all_to_all x1, waiting for transfers between devices, body(): shares = lax.all_to_all(partial.reshape(nz, ncl, vectors), 'z', 0, 0)  9.03 us
    ppermute x2, starting transfers between devices, shifted(): lax.ppermute(head, axis, [(i + 1, i) for i in range(ends)])  6.78 us
    all_to_all x1, starting transfers between devices, body(): shares = lax.all_to_all(partial.reshape(nz, ncl, vectors), 'z', 0, 0)  5.2 us
  transfers between devices with their start and end apart: 7, of which 3 were waited for; matrix products, arithmetic and copies ran while one was open for 13% of the time, Pallas kernels for 0%

profile of v1, /device:TPU:1, one launch (start us, length us, event | category | flops | bytes accessed | tf_op | source)
XLA Modules:
  0.0 92.5 jit_solution(14835671609302443058)
XLA Ops:
  0.0 1.2 %convert_element_type.22 = bf16[16,112,128]{2,1,0:T(8,128)(2,1)S(1)} convert(f32[16,112,128]{2,1,0:T(8,128)} %param.6) | non-fusion elementwise | flops 229376 | bytes 1376256 | tf_op jit(solution)/shard_map/convert_element_type | solution.py:45
  1.3 4.6 %collective-permute-start = (bf16[16,8,128]{2,1,0:T(8,128)(2,1)S(1)}, bf16[16,8,128]{2,1,0:T(8,128)(2,1)S(1)}, u32[]{:S(2)}, u32[]{:S(2)}) collective-permute-start(bf16[16,8,128]{2,1,0:T(8,128)(2,1)S(1)} %get-tuple-element.7), channel_id=1, source_target_pairs={{0,1},{1,2},{2,3},{3,4},{4,5},{5,6},{6,7},{7,8},{8,9},{9,10},{10,1... | collective-permute-start | bytes 98312 | tf_op jit(solution)/shard_map/ppermute | solution.py:19
  5.9 5.5 %collective-permute-start.1 = (bf16[16,8,128]{2,1,0:T(8,128)(2,1)S(1)}, bf16[16,8,128]{2,1,0:T(8,128)(2,1)S(1)}, u32[]{:S(2)}, u32[]{:S(2)}) collective-permute-start(bf16[16,8,128]{2,1,0:T(8,128)(2,1)S(1)} %get-tuple-element.8), channel_id=1, source_target_pairs={{1,0},{2,1},{3,2},{4,3},{5,4},{6,5},{7,6},{8,7},{9,8},{10,9},{11,1... | collective-permute-start | bytes 98312 | tf_op jit(solution)/shard_map/ppermute | solution.py:21
  11.4 1.0 %copy.40 = s32[32,16,4]{2,1,0:T(8,128)S(1)} copy(s32[32,16,4]{0,2,1:T(4,128)} %param.10) | data formatting | bytes 16384 | tf_op args[4]
  12.3 0.2 eq.47
  12.5 0.0 copy-start.2
  12.5 0.0 copy-start.3
  12.5 0.0 copy-start
  12.5 0.0 copy-start.1
  12.5 4.0 %fusion.14 = bf16[16,4,128]{2,1,0:T(4,128)(2,1)} fusion(s32[2048]{0:T(1024)S(1)} %eq.47, f32[4,2048]{1,0:T(4,128)} %param.11), kind=kOutput, calls=%fused_computation.14 | convolution fusion | flops 37765120 | bytes 57344 | tf_op jit(solution)/shard_map/dot_general | solution.py:50
  16.5 11.4 %all-to-all-start = ((bf16[16,4,128]{2,1,0:T(4,128)(2,1)}), bf16[16,4,128]{2,1,0:T(4,128)(2,1)S(1)}, u32[]{:S(2)}, u32[]{:S(2)}) async-start(bf16[16,4,128]{2,1,0:T(4,128)(2,1)} %fusion.14), calls=%async_computation | async-start | bytes 32768 | tf_op jit(solution)/shard_map/all_to_all | solution.py:52
  27.9 0.0 copy-done.2
  27.9 0.1 copy.38
  28.0 0.0 copy-done.3
  28.0 0.1 slice.27
  28.1 0.1 reshape.137
  28.2 0.2 copy.39
  28.4 0.2 reshape.138
  28.5 0.0 copy-done
  28.6 0.0 copy-done.1
  28.6 0.9 fusion.15
  29.5 0.1 copy.37
  29.6 0.1 reshape_squeeze.6
  29.7 0.1 copy.36
  29.8 0.0 collective-permute-done
  29.8 0.0 collective-permute-done.1
  29.8 0.1 pad_maximum_fusion.2
  29.8 9.4 %all-to-all-done = bf16[16,4,128]{2,1,0:T(4,128)(2,1)S(1)} async-done(((bf16[16,4,128]{2,1,0:T(4,128)(2,1)}), bf16[16,4,128]{2,1,0:T(4,128)(2,1)S(1)}, u32[]{:S(2)}, u32[]{:S(2)}) %all-to-all-start) | async-done | bytes 16416 | tf_op jit(solution)/shard_map/all_to_all | solution.py:52
  39.3 0.5 convolution_convert_fusion
  39.7 0.9 pad_maximum_fusion.1
  40.6 10.0 %all-to-all-start.1 = ((bf16[32,68,128]{2,1,0:T(8,128)(2,1)}), bf16[32,68,128]{2,1,0:T(8,128)(2,1)S(1)}, u32[]{:S(2)}, u32[]{:S(2)}) async-start(bf16[32,68,128]{2,1,0:T(8,128)(2,1)} %pad_maximum_fusion.1), calls=%async_computation.1 | async-start | bytes 1179648 | tf_op jit(solution)/shard_map/all_to_all | solution.py:64
  50.7 4.8 %collective-permute-start.2 = (bf16[8,128,128]{2,1,0:T(8,128)(2,1)S(1)}, bf16[8,128,128]{2,1,0:T(8,128)(2,1)S(1)}, u32[]{:S(2)}, u32[]{:S(2)}) collective-permute-start(bf16[8,128,128]{2,1,0:T(8,128)(2,1)S(1)} %get-tuple-element.5), channel_id=1, source_target_pairs={{0,16},{16,32},{32,48},{48,64},{64,80},{80,96},{96,112},{112,128},... | collective-permute-start | bytes 786440 | tf_op jit(solution)/shard_map/ppermute | solution.py:19
  55.5 1.3 %collective-permute-start.3 = (bf16[8,128,128]{2,1,0:T(8,128)(2,1)S(1)}, bf16[8,128,128]{2,1,0:T(8,128)(2,1)S(1)}, u32[]{:S(2)}, u32[]{:S(2)}) collective-permute-start(bf16[8,128,128]{2,1,0:T(8,128)(2,1)S(1)} %get-tuple-element.6), channel_id=1, source_target_pairs={{16,0},{32,16},{48,32},{64,48},{80,64},{96,80},{112,96},{128,112},... | collective-permute-start | bytes 786440 | tf_op jit(solution)/shard_map/ppermute | solution.py:21
  56.8 13.4 %collective-permute-done.2 = bf16[8,128,128]{2,1,0:T(8,128)(2,1)S(1)} collective-permute-done((bf16[8,128,128]{2,1,0:T(8,128)(2,1)S(1)}, bf16[8,128,128]{2,1,0:T(8,128)(2,1)S(1)}, u32[]{:S(2)}, u32[]{:S(2)}) %collective-permute-start.2) | collective-permute-done | bytes 262176 | tf_op jit(solution)/shard_map/ppermute | solution.py:19
  70.2 0.0 collective-permute-done.3
  70.2 0.1 pad_maximum_fusion
  70.3 2.0 %gather_fusion = bf16[48,128,128]{2,1,0:T(8,128)(2,1)} fusion(bf16[32,128,128]{2,1,0:T(8,128)(2,1)S(1)} %pad_maximum_fusion, s32[1024]{0:T(1024)S(1)} %pad_clamp_fusion), kind=kCustom, calls=%fused_computation | custom fusion | bytes 3145920 | tf_op jit(solution)/shard_map/jit(_take)/gather | solution.py:30
  72.3 0.0 all-to-all-done.1
  72.3 0.1 slice_reduce_fusion
  72.4 0.1 fusion.20
  72.5 0.6 copy.44
  73.1 5.2 %all-to-all-start.2 = ((f32[16,4,128]{2,1,0:T(4,128)}), f32[16,4,128]{2,1,0:T(4,128)S(1)}, u32[]{:S(2)}, u32[]{:S(2)}) async-start(f32[16,4,128]{2,1,0:T(4,128)} %copy.44), calls=%async_computation.2 | async-start | bytes 65536 | tf_op jit(solution)/shard_map/all_to_all | solution.py:68
  78.3 2.5 %fusion.8 = f32[16,128,128]{2,1,0:T(8,128)S(1)} fusion(bf16[16,3,128,128]{3,2,1,0:T(8,128)(2,1)} %bitcast.49, pred[16,3]{1,0:T(8,128)(4,1)S(1)} %copy.36, bf16[1,1,32,3,128,128]{5,4,3,2,1,0:T(8,128)(2,1)} %param.8), kind=kOutput, calls=%fused_computation.11 | convolution fusion | flops 202113024 | bytes 4194352 | tf_op jit(solution)/shard_map/ikyz,ikzr->iyr/dot_general | solution.py:31
  80.9 9.0 %all-to-all-done.2 = f32[16,4,128]{2,1,0:T(4,128)S(1)} async-done(((f32[16,4,128]{2,1,0:T(4,128)}), f32[16,4,128]{2,1,0:T(4,128)S(1)}, u32[]{:S(2)}, u32[]{:S(2)}) %all-to-all-start.2) | async-done | bytes 32800 | tf_op jit(solution)/shard_map/all_to_all | solution.py:68
  89.9 2.5 %fusion.13 = f32[16,112,128]{2,1,0:T(8,128)} fusion(f32[16,128,128]{2,1,0:T(8,128)S(1)} %fusion.8, f32[4,16,112]{2,1,0:T(8,128)S(1)} %copy-done.1, f32[4,128]{1,0:T(4,128)S(1)} %reduce_sum.22), kind=kOutput, calls=%fused_computation.13 | convolution fusion | flops 11239424 | bytes 1865728 | tf_op jit(solution)/shard_map/lxy,lr->xyr/dot_general | solution.py:70
  (9 shorter events, 0.1 us)
Async XLA Ops:
  1.3 28.5 %collective-permute-start = (bf16[16,8,128]{2,1,0:T(8,128)(2,1)S(1)}, bf16[16,8,128]{2,1,0:T(8,128)(2,1)S(1)}, u32[]{:S(2)}, u32[]{:S(2)}) collective-permute-start(bf16[16,8,128]{2,1,0:T(8,128)(2,1)S(1)} %get-tuple-element.7), channel_id=1, source_target_pairs={{0,1},{1,2},{2,3},{3,4},{4,5},{5,6},{6,7},{7,8},{8,9},{9,10},{10,1... | collective-permute-start | bytes 98312 | tf_op jit(solution)/shard_map/ppermute | solution.py:19
  5.9 23.9 %collective-permute-start.1 = (bf16[16,8,128]{2,1,0:T(8,128)(2,1)S(1)}, bf16[16,8,128]{2,1,0:T(8,128)(2,1)S(1)}, u32[]{:S(2)}, u32[]{:S(2)}) collective-permute-start(bf16[16,8,128]{2,1,0:T(8,128)(2,1)S(1)} %get-tuple-element.8), channel_id=1, source_target_pairs={{1,0},{2,1},{3,2},{4,3},{5,4},{6,5},{7,6},{8,7},{9,8},{10,9},{11,1... | collective-permute-start | bytes 98312 | tf_op jit(solution)/shard_map/ppermute | solution.py:21
  12.5 15.4 %copy-start.2 = (s32[32,16,4]{0,2,1:T(4,128)S(1)}, s32[32,16,4]{0,2,1:T(4,128)}, u32[]{:S(2)}) copy-start(s32[32,16,4]{0,2,1:T(4,128)} %param.10) | copy-start | bytes 24580
  12.5 15.5 %copy-start.3 = (s32[1,1,32,3]{2,1,3,0:T(1,128)S(1)}, s32[1,1,32,3]{2,1,3,0:T(1,128)}, u32[]{:S(2)}) copy-start(s32[1,1,32,3]{2,1,3,0:T(1,128)} %param.9) | copy-start | bytes 1156
  12.5 16.0 %copy-start = (f32[16,112,128]{2,1,0:T(8,128)S(1)}, f32[16,112,128]{2,1,0:T(8,128)}, u32[]{:S(2)}) copy-start(f32[16,112,128]{2,1,0:T(8,128)} %param.6) | copy-start | bytes 2752516
  12.5 16.0 %copy-start.1 = (f32[4,16,112]{2,1,0:T(8,128)S(1)}, f32[4,16,112]{2,1,0:T(8,128)}, u32[]{:S(2)}) copy-start(f32[4,16,112]{2,1,0:T(8,128)} %param.7) | copy-start | bytes 86020
  16.5 22.7 %all-to-all-start = ((bf16[16,4,128]{2,1,0:T(4,128)(2,1)}), bf16[16,4,128]{2,1,0:T(4,128)(2,1)S(1)}, u32[]{:S(2)}, u32[]{:S(2)}) async-start(bf16[16,4,128]{2,1,0:T(4,128)(2,1)} %fusion.14), calls=%async_computation | async-start | bytes 32768 | tf_op jit(solution)/shard_map/all_to_all | solution.py:52
  40.6 31.7 %all-to-all-start.1 = ((bf16[32,68,128]{2,1,0:T(8,128)(2,1)}), bf16[32,68,128]{2,1,0:T(8,128)(2,1)S(1)}, u32[]{:S(2)}, u32[]{:S(2)}) async-start(bf16[32,68,128]{2,1,0:T(8,128)(2,1)} %pad_maximum_fusion.1), calls=%async_computation.1 | async-start | bytes 1179648 | tf_op jit(solution)/shard_map/all_to_all | solution.py:64
  50.7 19.5 %collective-permute-start.2 = (bf16[8,128,128]{2,1,0:T(8,128)(2,1)S(1)}, bf16[8,128,128]{2,1,0:T(8,128)(2,1)S(1)}, u32[]{:S(2)}, u32[]{:S(2)}) collective-permute-start(bf16[8,128,128]{2,1,0:T(8,128)(2,1)S(1)} %get-tuple-element.5), channel_id=1, source_target_pairs={{0,16},{16,32},{32,48},{48,64},{64,80},{80,96},{96,112},{112,128},... | collective-permute-start | bytes 786440 | tf_op jit(solution)/shard_map/ppermute | solution.py:19
  55.5 14.7 %collective-permute-start.3 = (bf16[8,128,128]{2,1,0:T(8,128)(2,1)S(1)}, bf16[8,128,128]{2,1,0:T(8,128)(2,1)S(1)}, u32[]{:S(2)}, u32[]{:S(2)}) collective-permute-start(bf16[8,128,128]{2,1,0:T(8,128)(2,1)S(1)} %get-tuple-element.6), channel_id=1, source_target_pairs={{16,0},{32,16},{48,32},{64,48},{80,64},{96,80},{112,96},{128,112},... | collective-permute-start | bytes 786440 | tf_op jit(solution)/shard_map/ppermute | solution.py:21
  73.1 16.8 %all-to-all-start.2 = ((f32[16,4,128]{2,1,0:T(4,128)}), f32[16,4,128]{2,1,0:T(4,128)S(1)}, u32[]{:S(2)}, u32[]{:S(2)}) async-start(f32[16,4,128]{2,1,0:T(4,128)} %copy.44), calls=%async_computation.2 | async-start | bytes 65536 | tf_op jit(solution)/shard_map/all_to_all | solution.py:68

commit v2 on v1

v2 whole, which is shorter than its diff:
```python
import functools

import jax
import jax.numpy as jnp
from jax import lax
from jax.experimental import pallas as pl
from jax.experimental.pallas import tpu as pltpu
from jax.sharding import Mesh, PartitionSpec as P

W = 8
K = 3
NCL = 4
BF = jnp.bfloat16
F32 = jnp.float32
HIGH = lax.Precision.HIGHEST
VMEM = pl.BlockSpec(memory_space=pltpu.VMEM)
ANYWHERE = pl.BlockSpec(memory_space=pl.ANY)
LARGE = pltpu.CompilerParams(vmem_limit_bytes=60 * 1024 * 1024)
SLOW = pl.CostEstimate(flops=20_000_000_000, bytes_accessed=1_000_000, transcendentals=0)
GRANT = pltpu.CompilerParams(vmem_limit_bytes=32 * 1024 * 1024)


def order_kernel(rows_hbm, map_hbm, out_ref, rows_ref, map_ref, sems):
    fetch_map = pltpu.make_async_copy(map_hbm, map_ref, sems.at[0])
    fetch_rows = pltpu.make_async_copy(rows_hbm, rows_ref, sems.at[1])
    fetch_map.start()
    fetch_rows.start()
    ncl, total = rows_ref.shape
    ny, _, nx = map_ref.shape
    lanes = ncl * nx
    half = lanes // 2
    chunks = total // lanes
    fetch_map.wait()
    flat = jnp.concatenate([map_ref[:, m, :] for m in range(ncl)], axis=1)
    to = lax.broadcasted_iota(jnp.int32, (lanes, lanes), 1)
    h, zm = to // half, to % half
    source = (zm % ncl) * nx + (zm // ncl) * 2 + h
    swap = (lax.broadcasted_iota(jnp.int32, (lanes, lanes), 0) == source).astype(F32).astype(BF)
    upper_bits = (flat // 16).astype(F32).astype(BF)
    lower_bits = (flat % 16).astype(F32).astype(BF)
    ids = jnp.dot(upper_bits, swap, preferred_element_type=F32) * 16.0
    ids = (ids + jnp.dot(lower_bits, swap, preferred_element_type=F32)).astype(jnp.int32)
    fetch_rows.wait()
    upper = lax.broadcasted_iota(jnp.int32, (2 * ncl, lanes), 0) < ncl
    twice = [
        jnp.concatenate([rows_ref[:, s * lanes : (s + 1) * lanes]] * 2, axis=0) for s in range(chunks)
    ]
    done = []
    for pair in range(ny // 2):
        one, two = (jnp.broadcast_to(ids[2 * pair + i : 2 * pair + i + 1, :], upper.shape) for i in (0, 1))
        spot = jnp.where(upper, one, two)
        lane = spot % lanes
        chunk = spot // lanes
        picked = jnp.zeros(upper.shape, F32)
        for s in range(chunks):
            moved = jnp.take_along_axis(twice[s], lane, axis=1, mode="promise_in_bounds")
            picked = jnp.where(chunk == s, moved, picked)
        done.append(picked)
    picked = jnp.concatenate(done, axis=0)
    both = jnp.concatenate([picked, pltpu.roll(picked, half, 1)], axis=0)
    out_ref[...] = both.astype(BF)


def order_columns(rows, by_y):
    ny, ncl, nx = by_y.shape
    return pl.pallas_call(
        order_kernel,
        out_shape=jax.ShapeDtypeStruct((2 * ny * ncl, nx * ncl), BF),
        in_specs=[ANYWHERE, ANYWHERE],
        out_specs=VMEM,
        scratch_shapes=[
            pltpu.VMEM(rows.shape, F32),
            pltpu.VMEM(by_y.shape, jnp.int32),
            pltpu.SemaphoreType.DMA((2,)),
        ],
        compiler_params=LARGE,
    )(rows, by_y)


def route_kernel(held_ref, place_ref, contrib_ref, out_ref):
    held = held_ref.shape[0]
    slots = place_ref.shape[1]
    ncl = contrib_ref.shape[0]
    depth = out_ref.shape[1] - 2 * ncl
    turned = held_ref[...].astype(F32).T[:depth].astype(BF)
    rows = lax.broadcasted_iota(jnp.int32, (held, slots), 0)
    contrib = contrib_ref[...]
    coarse = contrib.astype(BF).astype(F32)
    both = jnp.concatenate([coarse, contrib - coarse], axis=0).astype(BF)
    for z in range(place_ref.shape[0]):
        pick = (rows == place_ref[z : z + 1, :]).astype(F32).astype(BF)
        sent = jnp.dot(turned, pick, preferred_element_type=F32)
        out_ref[z, 0:depth, :] = sent.astype(BF)
        out_ref[z, depth : depth + 2 * ncl, :] = both


def route(held, place, contrib):
    nz, slots = place.shape
    return pl.pallas_call(
        route_kernel,
        out_shape=jax.ShapeDtypeStruct((nz, (nz + 2) * contrib.shape[0], slots), BF),
        in_specs=[VMEM, VMEM, VMEM],
        out_specs=VMEM,
        compiler_params=GRANT,
        cost_estimate=SLOW,
    )(held, place, contrib)


def apply_kernel(got_ref, out_ref):
    nz, rows, lanes = got_ref.shape
    ncl = NCL
    depth = rows - 2 * ncl
    block = got_ref[0, 0:depth, :].astype(F32)
    for z in range(1, nz):
        block += got_ref[z, 0:depth, :].astype(F32)
    upper = lax.broadcasted_iota(jnp.int32, (2 * ncl, lanes), 0) < ncl
    high, low = [], []
    for q in range(nz // 2):
        one = got_ref[2 * q, depth:rows, :].astype(F32)
        two = got_ref[2 * q + 1, depth:rows, :].astype(F32)
        high.append(jnp.where(upper, one, pltpu.roll(two, ncl, 0)))
        low.append(jnp.where(upper, pltpu.roll(one, ncl, 0), two))
    turned = block.T.astype(BF)
    cells = jnp.concatenate(high + low, axis=0).astype(BF)
    out_ref[...] = jnp.dot(
        jnp.concatenate([turned, turned], axis=1), cells, preferred_element_type=F32
    )


def apply_block(got):
    slots = got.shape[2]
    return pl.pallas_call(
        apply_kernel,
        out_shape=jax.ShapeDtypeStruct((slots, slots), F32),
        in_specs=[VMEM],
        out_specs=VMEM,
        compiler_params=GRANT,
        cost_estimate=SLOW,
    )(got)


def round_kernel(cells_ref, after_ref, out_ref):
    out_ref[...] = cells_ref[...].astype(BF)


def round_cells(cells, after):
    block = pl.BlockSpec((cells.shape[0] // 4,) + cells.shape[1:], lambda i: (i, 0, 0))
    return pl.pallas_call(
        round_kernel,
        grid=(4,),
        out_shape=jax.ShapeDtypeStruct(cells.shape, BF),
        in_specs=[block, ANYWHERE],
        out_specs=block,
        compiler_params=GRANT,
    )(cells, after)


def widen_kernel(below_ref, mid_ref, above_ref, first_ref, last_ref):
    rows = first_ref.shape[0]
    for start, out_ref in ((0, first_ref), (rows, last_ref)):
        part = slice(start, start + rows)
        out_ref[...] = jnp.concatenate([below_ref[part], mid_ref[part], above_ref[part]], axis=1)


def widen(below, mid, above):
    wide = below.shape[1] + mid.shape[1] + above.shape[1]
    shape = jax.ShapeDtypeStruct((mid.shape[0] // 2, wide, mid.shape[2]), BF)
    return pl.pallas_call(
        widen_kernel,
        out_shape=(shape, shape),
        in_specs=[VMEM, VMEM, VMEM],
        out_specs=(VMEM, VMEM),
        compiler_params=GRANT,
    )(below, mid, above)


def solve_kernel(pattern_ref, left_ref, first_ref, last_ref, right_ref, inv_ref, after_ref, out_ref, ext_ref):
    step = pl.program_id(0)
    each = out_ref.shape[0]
    own_y = out_ref.shape[1]
    rows = left_ref.shape[0]

    @pl.when(step == 0)
    def _():
        for i, ref in enumerate((left_ref, first_ref, last_ref, right_ref)):
            ext_ref[i * rows : (i + 1) * rows] = ref[...]

    for i in range(each):
        spot = (W + step * each + i) * K
        blocks = jnp.concatenate([inv_ref[0, 0, i, k] for k in range(K)], axis=1)
        cells = jnp.concatenate([ext_ref[pattern_ref[spot + k]] for k in range(K)], axis=0)
        solved = jnp.dot(blocks, cells, preferred_element_type=F32)
        out_ref[i] = solved[W : W + own_y]


def solve(pattern, left, first, last, right, inv_blocks, after, own_y):
    steps = 4
    own_x = 2 * first.shape[0]
    each = own_x // steps
    wide, vectors = first.shape[1:]
    return pl.pallas_call(
        solve_kernel,
        grid_spec=pltpu.PrefetchScalarGridSpec(
            num_scalar_prefetch=1,
            grid=(steps,),
            in_specs=[
                VMEM,
                VMEM,
                VMEM,
                VMEM,
                pl.BlockSpec((1, 1, each, K, wide, wide), lambda i, p: (0, 0, i + W // each, 0, 0, 0)),
                ANYWHERE,
            ],
            out_specs=pl.BlockSpec((each, own_y, vectors), lambda i, p: (i, 0, 0)),
            scratch_shapes=[pltpu.VMEM((2 * own_x, wide, vectors), BF)],
        ),
        out_shape=jax.ShapeDtypeStruct((own_x, own_y, vectors), F32),
        compiler_params=GRANT,
    )(pattern, left, first, last, right, inv_blocks, after)


def finish_kernel(shares_ref, basis_ref, local_ref, out_ref):
    nz, ncl, lanes = shares_ref.shape
    each = out_ref.shape[0]
    start = pl.program_id(0) * each
    sol = shares_ref[0]
    for z in range(1, nz):
        sol += shares_ref[z]
    high = sol.astype(BF).astype(F32)
    terms = jnp.concatenate([high, sol - high, high, jnp.zeros((lanes - 3 * ncl, lanes), F32)], axis=0)
    terms = terms.astype(BF)
    for x in range(each):
        out_ref[x] = local_ref[start + x] + jnp.dot(basis_ref[start + x], terms, preferred_element_type=F32)


def finish(shares, basis, local):
    return pl.pallas_call(
        finish_kernel,
        grid=(4,),
        out_shape=jax.ShapeDtypeStruct(local.shape, F32),
        in_specs=[VMEM, VMEM, VMEM],
        out_specs=pl.BlockSpec((local.shape[0] // 4,) + local.shape[1:], lambda i: (i, 0, 0)),
        compiler_params=GRANT,
    )(shares, basis, local)


def neighbours(tail, head, axis):
    ends = lax.axis_size(axis) - 1
    return (
        lax.ppermute(tail, axis, [(i, i + 1) for i in range(ends)]),
        lax.ppermute(head, axis, [(i + 1, i) for i in range(ends)]),
    )


def body(residual, basis, inv_blocks, pattern, coarse_map, coarse_inv):
    nz = lax.axis_size("z")
    plane = lax.axis_size("h") * lax.axis_size("py")
    ncl, own_x, own_y = basis.shape
    vectors = residual.shape[2]
    slots = plane * ncl
    depth = nz * ncl

    columns = order_columns(coarse_inv, coarse_map.transpose(1, 2, 0))
    columns = columns.reshape(plane, ncl, 2 * depth)
    held = lax.all_to_all(columns, ("h", "py"), 0, 0).reshape(slots, 2 * depth)

    wanted = coarse_map.reshape(nz, slots)
    place = jnp.where(wanted // slots == lax.axis_index("z"), wanted % slots, -1)
    contrib = jnp.einsum("lxy,xyr->lr", basis, residual, precision=HIGH)
    sent = route(held, place, contrib)

    rounded = round_cells(residual, sent)
    below, above = neighbours(rounded[:, own_y - W :], rounded[:, :W], "py")
    first, last = widen(below, rounded, above)
    left, right = neighbours(last, first, ("z", "h"))
    partial = apply_block(lax.all_to_all(sent, "z", 0, 0))
    shares = lax.all_to_all(partial.reshape(plane, ncl, vectors), ("h", "py"), 0, 0)
    local_part = solve(pattern.reshape(-1), left, first, last, right, inv_blocks, partial, own_y)
    high = basis.astype(BF)
    low = (basis - high.astype(F32)).astype(BF)
    terms = jnp.concatenate([high, high, low], axis=0).transpose(1, 2, 0)
    terms = jnp.pad(terms, ((0, 0), (0, 0), (0, vectors - 3 * ncl)))
    return finish(shares, terms, local_part)


def solution(mesh):
    count_x, count_y = mesh.devices.shape
    fine = Mesh(mesh.devices.reshape(count_x // 2, 2, count_y), ("z", "h", "py"))
    px = ("z", "h")
    return jax.shard_map(
        body,
        mesh=fine,
        in_specs=(
            P(px, "py", None),
            P(None, px, "py"),
            P(px, "py", None, None, None, None),
            P(px, "py", None, None),
            P(),
            P(("z", "h", "py"), None),
        ),
        out_specs=P(px, "py", None),
        check_vma=False,
    )
```

time: 93 us -> 68.1 us (0.73)
  waiting for transfers between devices: 31.8 us -> 10.2 us
  matrix products: 10.6 us -> 2.08 us
  Pallas kernels: 0 us -> 7.82 us
  other arithmetic: 2.44 us -> 0.03 us
  local copies, waits for them, and re-layouts: 4.67 us -> 3.6 us
  starting transfers between devices: 42.7 us -> 43.7 us
    all_to_all x3, waiting for transfers between devices: 18.5 us -> 7.09 us  [the longest x1 3.91 us: body(): held = lax.all_to_all(columns, ('h', 'py'), 0, 0).reshape(slots, 2 * depth)]
    ppermute x4, waiting for transfers between devices: 13.4 us -> 3.07 us  [the longest x2 3.07 us: neighbours(): lax.ppermute(head, axis, [(i + 1, i) for i in range(ends)])]
    dot_general x6 -> x1, matrix products: 10.6 us -> 2.08 us  [body(): contrib = jnp.einsum('lxy,xyr->lr', basis, residual, precision=HIGH)]
    pallas_call x0 -> x7, Pallas kernels: none -> 7.82 us  [the longest x1 2.05 us: finish(): pl.pallas_call(finish_kernel, grid=(4,), out_shape=jax.ShapeDtypeStruct(l...]
    all_to_all x3, starting transfers between devices: 26.5 us -> 33.7 us  [the longest x1 13 us: body(): partial = apply_block(lax.all_to_all(sent, 'z', 0, 0))]
    ppermute x4, starting transfers between devices: 16.2 us -> 9.97 us  [the longest x2 6.76 us: neighbours(): lax.ppermute(tail, axis, [(i, i + 1) for i in range(ends)])]
    gather x1 -> x0, local copies, waits for them, and re-layouts: 1.95 us -> none  [local_solve(): jnp.take(ext, wanted.reshape(-1), axis=0)]
    unnamed x10, local copies, waits for them, and re-layouts: 1.06 us -> 2.94 us
  transfers between devices with their start and end apart: 7 -> 7, of which waited for: 3 -> 4; matrix products, arithmetic and copies ran while one was open for 13% -> 6% of each run, Pallas kernels for 0% -> 4%
where the time goes in v2:
time: 68.1 us; the launch traced here: 67.6 us
  starting transfers between devices  43.7 us (64%)
  waiting for transfers between devices  10.2 us (15%)
  Pallas kernels  7.82 us (11%)
  local copies, waits for them, and re-layouts  3.6 us (5%)
  matrix products  2.08 us (3%)
    all_to_all x1, starting transfers between devices, body(): partial = apply_block(lax.all_to_all(sent, 'z', 0, 0))  13 us
    all_to_all x1, starting transfers between devices, body(): held = lax.all_to_all(columns, ('h', 'py'), 0, 0).reshape(slots, 2 * depth)  10.4 us
    all_to_all x1, starting transfers between devices, body(): lax.all_to_all(partial.reshape(plane, ncl, vectors), ('h', 'py'), 0, 0)  10.3 us
    ppermute x2, starting transfers between devices, neighbours(): lax.ppermute(tail, axis, [(i, i + 1) for i in range(ends)])  6.76 us
    all_to_all x1, waiting for transfers between devices, body(): held = lax.all_to_all(columns, ('h', 'py'), 0, 0).reshape(slots, 2 * depth)  3.91 us
    ppermute x2, starting transfers between devices, neighbours(): lax.ppermute(head, axis, [(i + 1, i) for i in range(ends)])  3.21 us
    all_to_all x1, waiting for transfers between devices, body(): lax.all_to_all(partial.reshape(plane, ncl, vectors), ('h', 'py'), 0, 0)  3.07 us
    ppermute x2, waiting for transfers between devices, neighbours(): lax.ppermute(head, axis, [(i + 1, i) for i in range(ends)])  3.07 us
  transfers between devices with their start and end apart: 7, of which 4 were waited for; matrix products, arithmetic and copies ran while one was open for 6% of the time, Pallas kernels for 4%

profile of v2, /device:TPU:1, one launch (start us, length us, event | category | flops | bytes accessed | tf_op | source)
XLA Modules:
  0.0 67.6 jit_solution(4880505336226888151)
XLA Ops:
  0.0 1.9 %shard_map.64 = bf16[128,128]{1,0:T(8,128)(2,1)} custom-call(f32[4,2048]{1,0:T(4,128)} %rows_hbm.1, s32[16,4,32]{2,1,0:T(4,128)} %bitcast.12), custom_call_target="tpu_custom_call" | custom-call | tf_op jit(solution)/shard_map/pallas_call | solution.py:66
  1.9 10.4 %all-to-all-start = ((bf16[32,4,128]{2,1,0:T(4,128)(2,1)}), bf16[32,4,128]{2,1,0:T(4,128)(2,1)S(1)}, u32[]{:S(2)}, u32[]{:S(2)}) async-start(bf16[32,4,128]{2,1,0:T(4,128)(2,1)} %bitcast.13), calls=%async_computation | async-start | bytes 65536 | tf_op jit(solution)/shard_map/all_to_all | solution.py:265
  12.3 1.0 %copy.19 = s32[32,16,4]{2,1,0:T(8,128)S(1)} copy(s32[32,16,4]{0,2,1:T(4,128)} %param.10) | data formatting | bytes 16384 | tf_op args[4]
  13.2 0.2 reshape.17
  13.4 2.1 %convolution_bitcast_fusion.contrib_ref = f32[4,128]{1,0:T(4,128)S(1)} fusion(f32[16,112,128]{2,1,0:T(8,128)} %cells_ref.1, f32[4,16,112]{2,1,0:T(8,128)} %param.7), kind=kOutput, calls=%fused_computation | convolution fusion | flops 11010048 | bytes 948224 | tf_op jit(solution)/shard_map/lxy,xyr->lr/dot_general | solution.py:269
  15.5 3.9 %all-to-all-done = bf16[32,4,128]{2,1,0:T(4,128)(2,1)S(1)} async-done(((bf16[32,4,128]{2,1,0:T(4,128)(2,1)}), bf16[32,4,128]{2,1,0:T(4,128)(2,1)S(1)}, u32[]{:S(2)}, u32[]{:S(2)}) %all-to-all-start) | async-done | bytes 32800 | tf_op jit(solution)/shard_map/all_to_all | solution.py:265
  19.4 0.0 copy-start
  19.4 0.0 copy-start.2
  19.4 0.0 copy-start.3
  19.4 1.0 %shard_map.65.after_ref = bf16[16,72,128]{2,1,0:T(8,128)(2,1)} custom-call(bf16[128,128]{1,0:T(8,128)(2,1)S(1)} %bitcast.10, s32[16,128]{1,0:T(8,128)S(1)} %fusion.2.place_ref, f32[4,128]{1,0:T(4,128)S(1)} %convolution_bitcast_fusion.contrib_ref), custom_call_target="tpu_custom_call" | custom-call | flops 20000000000 | bytes 1000000 | tf_op jit(solution)/shard_map/pallas_call | solution.py:99
  20.4 13.0 %all-to-all-start.1 = ((bf16[16,72,128]{2,1,0:T(8,128)(2,1)}), bf16[16,72,128]{2,1,0:T(8,128)(2,1)S(1)}, u32[]{:S(2)}, u32[]{:S(2)}) async-start(bf16[16,72,128]{2,1,0:T(8,128)(2,1)} %shard_map.65.after_ref), calls=%async_computation.1 | async-start | bytes 589824 | tf_op jit(solution)/shard_map/all_to_all | solution.py:276
  33.5 0.0 copy-done
  33.5 0.1 shard_map.67.mid_ref
  33.6 3.1 %collective-permute-start = (bf16[16,8,128]{2,1,0:T(8,128)(2,1)S(1)}, bf16[16,8,128]{2,1,0:T(8,128)(2,1)S(1)}, u32[]{:S(2)}, u32[]{:S(2)}) collective-permute-start(bf16[16,8,128]{2,1,0:T(8,128)(2,1)S(1)} %get-tuple-element.12), channel_id=1, source_target_pairs={{0,1},{1,2},{2,3},{3,4},{4,5},{5,6},{6,7},{7,8},{8,9},{9,10},{10,1... | collective-permute-start | bytes 98312 | tf_op jit(solution)/shard_map/ppermute | solution.py:250
  36.7 1.9 %collective-permute-start.1 = (bf16[16,8,128]{2,1,0:T(8,128)(2,1)S(1)}, bf16[16,8,128]{2,1,0:T(8,128)(2,1)S(1)}, u32[]{:S(2)}, u32[]{:S(2)}) collective-permute-start(bf16[16,8,128]{2,1,0:T(8,128)(2,1)S(1)} %get-tuple-element.11), channel_id=1, source_target_pairs={{1,0},{2,1},{3,2},{4,3},{5,4},{6,5},{7,6},{8,7},{9,8},{10,9},{11,1... | collective-permute-start | bytes 98312 | tf_op jit(solution)/shard_map/ppermute | solution.py:251
  38.7 0.0 copy-done.2
  38.7 0.0 copy-done.3
  38.7 0.1 copy.22
  38.8 0.1 reshape.19.pattern_ref
  38.9 0.0 collective-permute-done.below_ref
  38.9 3.1 %collective-permute-done.1.above_ref = bf16[16,8,128]{2,1,0:T(8,128)(2,1)S(1)} collective-permute-done((bf16[16,8,128]{2,1,0:T(8,128)(2,1)S(1)}, bf16[16,8,128]{2,1,0:T(8,128)(2,1)S(1)}, u32[]{:S(2)}, u32[]{:S(2)}) %collective-permute-start.1) | collective-permute-done | bytes 32800 | tf_op jit(solution)/shard_map/ppermute | solution.py:251
  42.0 0.1 shard_map.68
  42.1 3.7 %collective-permute-start.2 = (bf16[8,128,128]{2,1,0:T(8,128)(2,1)S(1)}, bf16[8,128,128]{2,1,0:T(8,128)(2,1)S(1)}, u32[]{:S(2)}, u32[]{:S(2)}) collective-permute-start(bf16[8,128,128]{2,1,0:T(8,128)(2,1)S(1)} %get-tuple-element.7.last_ref), channel_id=1, source_target_pairs={{0,16},{16,32},{32,48},{48,64},{64,80},{80,96},{96,112},{112,128},... | collective-permute-start | bytes 786440 | tf_op jit(solution)/shard_map/ppermute | solution.py:250
  45.7 1.3 %collective-permute-start.3 = (bf16[8,128,128]{2,1,0:T(8,128)(2,1)S(1)}, bf16[8,128,128]{2,1,0:T(8,128)(2,1)S(1)}, u32[]{:S(2)}, u32[]{:S(2)}) collective-permute-start(bf16[8,128,128]{2,1,0:T(8,128)(2,1)S(1)} %get-tuple-element.8.first_ref), channel_id=1, source_target_pairs={{16,0},{32,16},{48,32},{64,48},{80,64},{96,80},{112,96},{128,112},... | collective-permute-start | bytes 786440 | tf_op jit(solution)/shard_map/ppermute | solution.py:251
  47.0 0.1 all-to-all-done.1.got_ref
  47.1 0.9 %shard_map.66.after_ref = f32[128,128]{1,0:T(8,128)} custom-call(bf16[16,72,128]{2,1,0:T(8,128)(2,1)S(1)} %all-to-all-done.1.got_ref), custom_call_target="tpu_custom_call" | custom-call | flops 20000000000 | bytes 1000000 | tf_op jit(solution)/shard_map/pallas_call | solution.py:132
  48.1 10.3 %all-to-all-start.2 = ((f32[32,4,128]{2,1,0:T(4,128)}), f32[32,4,128]{2,1,0:T(4,128)S(1)}, u32[]{:S(2)}, u32[]{:S(2)}) async-start(f32[32,4,128]{2,1,0:T(4,128)} %bitcast.4), calls=%async_computation.2 | async-start | bytes 131072 | tf_op jit(solution)/shard_map/all_to_all | solution.py:277
  58.4 0.3 copy.21
  58.7 0.1 pad.4.basis_ref
  58.8 0.0 collective-permute-done.2.left_ref
  58.8 0.0 collective-permute-done.3.right_ref
  58.8 0.0 copy-start.1
  58.8 1.9 %copy-done.1 = bf16[1,1,32,3,128,128]{5,4,3,2,1,0:T(8,128)(2,1)S(1)} copy-done((bf16[1,1,32,3,128,128]{5,4,3,2,1,0:T(8,128)(2,1)S(1)}, bf16[1,1,32,3,128,128]{5,4,3,2,1,0:T(8,128)(2,1)}, u32[]{:S(2)}) %copy-start.1) | copy-done | bytes 3145752
  60.7 1.7 %shard_map.69.local_ref = f32[16,112,128]{2,1,0:T(8,128)S(1)} custom-call(s32[96]{0:T(128)S(1)} %reshape.19.pattern_ref, bf16[8,128,128]{2,1,0:T(8,128)(2,1)S(1)} %collective-permute-done.2.left_ref, bf16[8,128,128]{2,1,0:T(8,128)(2,1)S(1)} %get-tuple-element.8.first_ref, bf16[8,128,128]{2,1,0:T(8,128)(2,1)S(1)} %get-tuple-element.7.last_ref, ...), custom_call_target="tpu_custom_call" | custom-call | tf_op jit(solution)/shard_map/pallas_call | solution.py:201
  62.4 3.1 %all-to-all-done.2.shares_ref = f32[32,4,128]{2,1,0:T(4,128)S(1)} async-done(((f32[32,4,128]{2,1,0:T(4,128)}), f32[32,4,128]{2,1,0:T(4,128)S(1)}, u32[]{:S(2)}, u32[]{:S(2)}) %all-to-all-start.2) | async-done | bytes 65568 | tf_op jit(solution)/shard_map/all_to_all | solution.py:277
  65.5 2.1 %shard_map.70 = f32[16,112,128]{2,1,0:T(8,128)} custom-call(f32[32,4,128]{2,1,0:T(4,128)S(1)} %all-to-all-done.2.shares_ref, bf16[16,112,128]{2,1,0:T(8,128)(2,1)S(1)} %pad.4.basis_ref, f32[16,112,128]{2,1,0:T(8,128)S(1)} %shard_map.69.local_ref), custom_call_target="tpu_custom_call" | custom-call | tf_op jit(solution)/shard_map/pallas_call | solution.py:237
  (4 shorter events, 0.0 us)
Async XLA Ops:
  1.9 17.5 %all-to-all-start = ((bf16[32,4,128]{2,1,0:T(4,128)(2,1)}), bf16[32,4,128]{2,1,0:T(4,128)(2,1)S(1)}, u32[]{:S(2)}, u32[]{:S(2)}) async-start(bf16[32,4,128]{2,1,0:T(4,128)(2,1)} %bitcast.13), calls=%async_computation | async-start | bytes 65536 | tf_op jit(solution)/shard_map/all_to_all | solution.py:265
  19.4 14.1 %copy-start = (f32[16,112,128]{2,1,0:T(8,128)S(1)}, f32[16,112,128]{2,1,0:T(8,128)}, u32[]{:S(2)}) copy-start(f32[16,112,128]{2,1,0:T(8,128)} %cells_ref.1) | copy-start | bytes 2752516
  19.4 19.3 %copy-start.2 = (f32[4,16,112]{2,1,0:T(8,128)S(1)}, f32[4,16,112]{2,1,0:T(8,128)}, u32[]{:S(2)}) copy-start(f32[4,16,112]{2,1,0:T(8,128)} %param.7) | copy-start | bytes 86020
  19.4 19.3 %copy-start.3 = (s32[1,1,32,3]{2,1,3,0:T(1,128)S(1)}, s32[1,1,32,3]{2,1,3,0:T(1,128)}, u32[]{:S(2)}) copy-start(s32[1,1,32,3]{2,1,3,0:T(1,128)} %param.9) | copy-start | bytes 1156
  20.4 26.7 %all-to-all-start.1 = ((bf16[16,72,128]{2,1,0:T(8,128)(2,1)}), bf16[16,72,128]{2,1,0:T(8,128)(2,1)S(1)}, u32[]{:S(2)}, u32[]{:S(2)}) async-start(bf16[16,72,128]{2,1,0:T(8,128)(2,1)} %shard_map.65.after_ref), calls=%async_computation.1 | async-start | bytes 589824 | tf_op jit(solution)/shard_map/all_to_all | solution.py:276
  33.6 5.3 %collective-permute-start = (bf16[16,8,128]{2,1,0:T(8,128)(2,1)S(1)}, bf16[16,8,128]{2,1,0:T(8,128)(2,1)S(1)}, u32[]{:S(2)}, u32[]{:S(2)}) collective-permute-start(bf16[16,8,128]{2,1,0:T(8,128)(2,1)S(1)} %get-tuple-element.12), channel_id=1, source_target_pairs={{0,1},{1,2},{2,3},{3,4},{4,5},{5,6},{6,7},{7,8},{8,9},{9,10},{10,1... | collective-permute-start | bytes 98312 | tf_op jit(solution)/shard_map/ppermute | solution.py:250
  36.7 5.2 %collective-permute-start.1 = (bf16[16,8,128]{2,1,0:T(8,128)(2,1)S(1)}, bf16[16,8,128]{2,1,0:T(8,128)(2,1)S(1)}, u32[]{:S(2)}, u32[]{:S(2)}) collective-permute-start(bf16[16,8,128]{2,1,0:T(8,128)(2,1)S(1)} %get-tuple-element.11), channel_id=1, source_target_pairs={{1,0},{2,1},{3,2},{4,3},{5,4},{6,5},{7,6},{8,7},{9,8},{10,9},{11,1... | collective-permute-start | bytes 98312 | tf_op jit(solution)/shard_map/ppermute | solution.py:251
  42.1 16.7 %collective-permute-start.2 = (bf16[8,128,128]{2,1,0:T(8,128)(2,1)S(1)}, bf16[8,128,128]{2,1,0:T(8,128)(2,1)S(1)}, u32[]{:S(2)}, u32[]{:S(2)}) collective-permute-start(bf16[8,128,128]{2,1,0:T(8,128)(2,1)S(1)} %get-tuple-element.7.last_ref), channel_id=1, source_target_pairs={{0,16},{16,32},{32,48},{48,64},{64,80},{80,96},{96,112},{112,128},... | collective-permute-start | bytes 786440 | tf_op jit(solution)/shard_map/ppermute | solution.py:250
  45.7 13.1 %collective-permute-start.3 = (bf16[8,128,128]{2,1,0:T(8,128)(2,1)S(1)}, bf16[8,128,128]{2,1,0:T(8,128)(2,1)S(1)}, u32[]{:S(2)}, u32[]{:S(2)}) collective-permute-start(bf16[8,128,128]{2,1,0:T(8,128)(2,1)S(1)} %get-tuple-element.8.first_ref), channel_id=1, source_target_pairs={{16,0},{32,16},{48,32},{64,48},{80,64},{96,80},{112,96},{128,112},... | collective-permute-start | bytes 786440 | tf_op jit(solution)/shard_map/ppermute | solution.py:251
  48.1 17.4 %all-to-all-start.2 = ((f32[32,4,128]{2,1,0:T(4,128)}), f32[32,4,128]{2,1,0:T(4,128)S(1)}, u32[]{:S(2)}, u32[]{:S(2)}) async-start(f32[32,4,128]{2,1,0:T(4,128)} %bitcast.4), calls=%async_computation.2 | async-start | bytes 131072 | tf_op jit(solution)/shard_map/all_to_all | solution.py:277
  58.8 1.9 %copy-start.1 = (bf16[1,1,32,3,128,128]{5,4,3,2,1,0:T(8,128)(2,1)S(1)}, bf16[1,1,32,3,128,128]{5,4,3,2,1,0:T(8,128)(2,1)}, u32[]{:S(2)}) copy-start(bf16[1,1,32,3,128,128]{5,4,3,2,1,0:T(8,128)(2,1)} %inv_ref.1) | copy-start | bytes 9437188

commit v3 on v2

--- a/solution.py
+++ b/solution.py
@@ -14,9 +14,11 @@
 F32 = jnp.float32
 HIGH = lax.Precision.HIGHEST
 VMEM = pl.BlockSpec(memory_space=pltpu.VMEM)
+HBM = pl.BlockSpec(memory_space=pltpu.HBM)
 ANYWHERE = pl.BlockSpec(memory_space=pl.ANY)
 LARGE = pltpu.CompilerParams(vmem_limit_bytes=60 * 1024 * 1024)
 SLOW = pl.CostEstimate(flops=20_000_000_000, bytes_accessed=1_000_000, transcendentals=0)
+SOLVE = pltpu.CompilerParams(vmem_limit_bytes=50 * 1024 * 1024)
 GRANT = pltpu.CompilerParams(vmem_limit_bytes=32 * 1024 * 1024)
 
 
@@ -30,12 +32,12 @@
     lanes = ncl * nx
     half = lanes // 2
     chunks = total // lanes
-    fetch_map.wait()
-    flat = jnp.concatenate([map_ref[:, m, :] for m in range(ncl)], axis=1)
     to = lax.broadcasted_iota(jnp.int32, (lanes, lanes), 1)
     h, zm = to // half, to % half
     source = (zm % ncl) * nx + (zm // ncl) * 2 + h
     swap = (lax.broadcasted_iota(jnp.int32, (lanes, lanes), 0) == source).astype(F32).astype(BF)
+    fetch_map.wait()
+    flat = jnp.concatenate([map_ref[:, m, :] for m in range(ncl)], axis=1)
     upper_bits = (flat // 16).astype(F32).astype(BF)
     lower_bits = (flat % 16).astype(F32).astype(BF)
     ids = jnp.dot(upper_bits, swap, preferred_element_type=F32) * 16.0
@@ -174,72 +176,81 @@
     )(below, mid, above)
 
 
-def solve_kernel(pattern_ref, left_ref, first_ref, last_ref, right_ref, inv_ref, after_ref, out_ref, ext_ref):
-    step = pl.program_id(0)
-    each = out_ref.shape[0]
-    own_y = out_ref.shape[1]
+def solve_kernel(pattern_ref, left_ref, first_ref, last_ref, right_ref, inv_hbm, after_ref, out_ref, ext_ref, inv_ref, sems):
+    own_x, own_y = out_ref.shape[:2]
     rows = left_ref.shape[0]
-
-    @pl.when(step == 0)
-    def _():
-        for i, ref in enumerate((left_ref, first_ref, last_ref, right_ref)):
-            ext_ref[i * rows : (i + 1) * rows] = ref[...]
-
-    for i in range(each):
-        spot = (W + step * each + i) * K
-        blocks = jnp.concatenate([inv_ref[0, 0, i, k] for k in range(K)], axis=1)
-        cells = jnp.concatenate([ext_ref[pattern_ref[spot + k]] for k in range(K)], axis=0)
-        solved = jnp.dot(blocks, cells, preferred_element_type=F32)
-        out_ref[i] = solved[W : W + own_y]
+    parts = sems.shape[0]
+    each = own_x // parts
+    fetches = [
+        pltpu.make_async_copy(
+            inv_hbm.at[0, 0, pl.ds(W + part * each, each)], inv_ref.at[pl.ds(part * each, each)], sems.at[part]
+        )
+        for part in range(parts)
+    ]
+    for fetch in fetches:
+        fetch.start()
+    for i, ref in enumerate((left_ref, first_ref, last_ref, right_ref)):
+        ext_ref[i * rows : (i + 1) * rows] = ref[...]
+    for part in range(parts):
+        fetches[part].wait()
+        for i in range(part * each, (part + 1) * each):
+            spot = (W + i) * K
+            blocks = jnp.concatenate([inv_ref[i, k] for k in range(K)], axis=1)
+            cells = jnp.concatenate([ext_ref[pattern_ref[spot + k]] for k in range(K)], axis=0)
+            solved = jnp.dot(blocks, cells, preferred_element_type=F32)
+            out_ref[i] = solved[W : W + own_y]
 
 
 def solve(pattern, left, first, last, right, inv_blocks, after, own_y):
-    steps = 4
+    parts = 4
     own_x = 2 * first.shape[0]
-    each = own_x // steps
     wide, vectors = first.shape[1:]
     return pl.pallas_call(
         solve_kernel,
-        grid_spec=pltpu.PrefetchScalarGridSpec(
-            num_scalar_prefetch=1,
-            grid=(steps,),
-            in_specs=[
-                VMEM,
-                VMEM,
-                VMEM,
-                VMEM,
-                pl.BlockSpec((1, 1, each, K, wide, wide), lambda i, p: (0, 0, i + W // each, 0, 0, 0)),
-                ANYWHERE,
-            ],
-            out_specs=pl.BlockSpec((each, own_y, vectors), lambda i, p: (i, 0, 0)),
-            scratch_shapes=[pltpu.VMEM((2 * own_x, wide, vectors), BF)],
-        ),
+        in_specs=[pl.BlockSpec(memory_space=pltpu.SMEM), VMEM, VMEM, VMEM, VMEM, HBM, ANYWHERE],
+        out_specs=VMEM,
+        scratch_shapes=[
+            pltpu.VMEM((2 * own_x, wide, vectors), BF),
+            pltpu.VMEM((own_x, K, wide, wide), BF),
+            pltpu.SemaphoreType.DMA((parts,)),
+        ],
         out_shape=jax.ShapeDtypeStruct((own_x, own_y, vectors), F32),
-        compiler_params=GRANT,
+        compiler_params=SOLVE,
     )(pattern, left, first, last, right, inv_blocks, after)
 
 
-def finish_kernel(shares_ref, basis_ref, local_ref, out_ref):
-    nz, ncl, lanes = shares_ref.shape
-    each = out_ref.shape[0]
-    start = pl.program_id(0) * each
-    sol = shares_ref[0]
-    for z in range(1, nz):
-        sol += shares_ref[z]
+def finish_kernel(shares_ref, basis_ref, local_ref, out_hbm, out_ref, sems):
+    ncl = NCL
+    tile, lanes = 2 * ncl, shares_ref.shape[1]
+    tiles = [shares_ref[i * tile : (i + 1) * tile, :] for i in range(shares_ref.shape[0] // tile)]
+    while len(tiles) > 1:
+        tiles = [tiles[i] + tiles[i + 1] for i in range(0, len(tiles), 2)]
+    sol = tiles[0] + pltpu.roll(tiles[0], ncl, 0)
     high = sol.astype(BF).astype(F32)
-    terms = jnp.concatenate([high, sol - high, high, jnp.zeros((lanes - 3 * ncl, lanes), F32)], axis=0)
-    terms = terms.astype(BF)
-    for x in range(each):
-        out_ref[x] = local_ref[start + x] + jnp.dot(basis_ref[start + x], terms, preferred_element_type=F32)
+    upper = lax.broadcasted_iota(jnp.int32, (tile, lanes), 0) < ncl
+    terms = [jnp.where(upper, high, sol - high), jnp.where(upper, high, 0.0)]
+    terms = jnp.concatenate(terms + [jnp.zeros((lanes - 2 * tile, lanes), F32)], axis=0).astype(BF)
+    parts = sems.shape[0]
+    each = out_ref.shape[0] // parts
+    stores = []
+    for part in range(parts):
+        for x in range(part * each, (part + 1) * each):
+            out_ref[x] = local_ref[x] + jnp.dot(basis_ref[x], terms, preferred_element_type=F32)
+        rows = pl.ds(part * each, each)
+        store = pltpu.make_async_copy(out_ref.at[rows], out_hbm.at[rows], sems.at[part])
+        store.start()
+        stores.append(store)
+    for store in stores:
+        store.wait()
 
 
 def finish(shares, basis, local):
     return pl.pallas_call(
         finish_kernel,
-        grid=(4,),
         out_shape=jax.ShapeDtypeStruct(local.shape, F32),
         in_specs=[VMEM, VMEM, VMEM],
-        out_specs=pl.BlockSpec((local.shape[0] // 4,) + local.shape[1:], lambda i: (i, 0, 0)),
+        out_specs=HBM,
+        scratch_shapes=[pltpu.VMEM(local.shape, F32), pltpu.SemaphoreType.DMA((8,))],
         compiler_params=GRANT,
     )(shares, basis, local)
 
@@ -276,11 +287,10 @@
     partial = apply_block(lax.all_to_all(sent, "z", 0, 0))
     shares = lax.all_to_all(partial.reshape(plane, ncl, vectors), ("h", "py"), 0, 0)
     local_part = solve(pattern.reshape(-1), left, first, last, right, inv_blocks, partial, own_y)
-    high = basis.astype(BF)
-    low = (basis - high.astype(F32)).astype(BF)
-    terms = jnp.concatenate([high, high, low], axis=0).transpose(1, 2, 0)
+    high = lax.reduce_precision(basis, 8, 7)
+    terms = jnp.concatenate([high, high, basis - high], axis=0).astype(BF).transpose(1, 2, 0)
     terms = jnp.pad(terms, ((0, 0), (0, 0), (0, vectors - 3 * ncl)))
-    return finish(shares, terms, local_part)
+    return finish(shares.reshape(slots, vectors), terms, local_part)
 
 
 def solution(mesh):

time: 68.1 us -> 67.2 us (0.987)
  local copies, waits for them, and re-layouts: 3.6 us -> 1.71 us
  waiting for transfers between devices: 10.2 us -> 11.1 us
    unnamed x10 -> x8, local copies, waits for them, and re-layouts: 2.94 us -> 1.05 us
    all_to_all x1, waiting for transfers between devices: 3.07 us -> 4.06 us  [body(): lax.all_to_all(partial.reshape(plane, ncl, vectors), ('h', 'py'), 0, 0)]
  transfers between devices with their start and end apart: 7 -> 7, of which waited for: 4 -> 4; matrix products, arithmetic and copies ran while one was open for 6% -> 6% of each run, Pallas kernels for 4% -> 6%
where the time goes in v3:
time: 67.2 us; the launch traced here: 66.7 us
  starting transfers between devices  43.7 us (65%)
  waiting for transfers between devices  11.1 us (17%)
  Pallas kernels  7.83 us (12%)
  matrix products  2.08 us (3%)
  local copies, waits for them, and re-layouts  1.71 us (3%)
    all_to_all x1, starting transfers between devices, body(): partial = apply_block(lax.all_to_all(sent, 'z', 0, 0))  13 us
    all_to_all x1, starting transfers between devices, body(): held = lax.all_to_all(columns, ('h', 'py'), 0, 0).reshape(slots, 2 * depth)  10.4 us
    all_to_all x1, starting transfers between devices, body(): lax.all_to_all(partial.reshape(plane, ncl, vectors), ('h', 'py'), 0, 0)  10.3 us
    ppermute x2, starting transfers between devices, neighbours(): lax.ppermute(tail, axis, [(i, i + 1) for i in range(ends)])  6.76 us
    all_to_all x1, waiting for transfers between devices, body(): lax.all_to_all(partial.reshape(plane, ncl, vectors), ('h', 'py'), 0, 0)  4.06 us
    all_to_all x1, waiting for transfers between devices, body(): held = lax.all_to_all(columns, ('h', 'py'), 0, 0).reshape(slots, 2 * depth)  3.91 us
    ppermute x2, starting transfers between devices, neighbours(): lax.ppermute(head, axis, [(i + 1, i) for i in range(ends)])  3.21 us
    ppermute x2, waiting for transfers between devices, neighbours(): lax.ppermute(head, axis, [(i + 1, i) for i in range(ends)])  3.07 us
  transfers between devices with their start and end apart: 7, of which 4 were waited for; matrix products, arithmetic and copies ran while one was open for 6% of the time, Pallas kernels for 6%

profile of v3, /device:TPU:1, one launch (start us, length us, event | category | flops | bytes accessed | tf_op | source)
XLA Modules:
  0.0 66.7 jit_solution(4999271842392976104)
XLA Ops:
  0.0 1.9 %shard_map.64 = bf16[128,128]{1,0:T(8,128)(2,1)} custom-call(f32[4,2048]{1,0:T(4,128)} %rows_hbm.1, s32[16,4,32]{2,1,0:T(4,128)} %bitcast.14), custom_call_target="tpu_custom_call" | custom-call | tf_op jit(solution)/shard_map/pallas_call | solution.py:68
  1.9 10.4 %all-to-all-start = ((bf16[32,4,128]{2,1,0:T(4,128)(2,1)}), bf16[32,4,128]{2,1,0:T(4,128)(2,1)S(1)}, u32[]{:S(2)}, u32[]{:S(2)}) async-start(bf16[32,4,128]{2,1,0:T(4,128)(2,1)} %bitcast.15), calls=%async_computation | async-start | bytes 65536 | tf_op jit(solution)/shard_map/all_to_all | solution.py:276
  12.3 1.0 %copy.17 = s32[32,16,4]{2,1,0:T(8,128)S(1)} copy(s32[32,16,4]{0,2,1:T(4,128)} %param.10) | data formatting | bytes 16384 | tf_op args[4]
  13.2 0.2 reshape.20
  13.4 2.1 %convolution_bitcast_fusion.contrib_ref = f32[4,128]{1,0:T(4,128)S(1)} fusion(f32[16,112,128]{2,1,0:T(8,128)} %cells_ref.1, f32[4,16,112]{2,1,0:T(8,128)} %param.7), kind=kOutput, calls=%fused_computation | convolution fusion | flops 11010048 | bytes 948224 | tf_op jit(solution)/shard_map/lxy,xyr->lr/dot_general | solution.py:280
  15.5 3.9 %all-to-all-done = bf16[32,4,128]{2,1,0:T(4,128)(2,1)S(1)} async-done(((bf16[32,4,128]{2,1,0:T(4,128)(2,1)}), bf16[32,4,128]{2,1,0:T(4,128)(2,1)S(1)}, u32[]{:S(2)}, u32[]{:S(2)}) %all-to-all-start) | async-done | bytes 32800 | tf_op jit(solution)/shard_map/all_to_all | solution.py:276
  19.4 0.0 copy-start
  19.4 0.0 copy-start.1
  19.4 0.0 copy-start.2
  19.4 1.0 %shard_map.65.after_ref = bf16[16,72,128]{2,1,0:T(8,128)(2,1)} custom-call(bf16[128,128]{1,0:T(8,128)(2,1)S(1)} %bitcast.12, s32[16,128]{1,0:T(8,128)S(1)} %fusion.3.place_ref, f32[4,128]{1,0:T(4,128)S(1)} %convolution_bitcast_fusion.contrib_ref), custom_call_target="tpu_custom_call" | custom-call | flops 20000000000 | bytes 1000000 | tf_op jit(solution)/shard_map/pallas_call | solution.py:101
  20.4 13.0 %all-to-all-start.1 = ((bf16[16,72,128]{2,1,0:T(8,128)(2,1)}), bf16[16,72,128]{2,1,0:T(8,128)(2,1)S(1)}, u32[]{:S(2)}, u32[]{:S(2)}) async-start(bf16[16,72,128]{2,1,0:T(8,128)(2,1)} %shard_map.65.after_ref), calls=%async_computation.1 | async-start | bytes 589824 | tf_op jit(solution)/shard_map/all_to_all | solution.py:287
  33.5 0.0 copy-done
  33.5 0.1 shard_map.67.mid_ref
  33.6 3.1 %collective-permute-start = (bf16[16,8,128]{2,1,0:T(8,128)(2,1)S(1)}, bf16[16,8,128]{2,1,0:T(8,128)(2,1)S(1)}, u32[]{:S(2)}, u32[]{:S(2)}) collective-permute-start(bf16[16,8,128]{2,1,0:T(8,128)(2,1)S(1)} %get-tuple-element.10), channel_id=1, source_target_pairs={{0,1},{1,2},{2,3},{3,4},{4,5},{5,6},{6,7},{7,8},{8,9},{9,10},{10,1... | collective-permute-start | bytes 98312 | tf_op jit(solution)/shard_map/ppermute | solution.py:261
  36.7 1.9 %collective-permute-start.1 = (bf16[16,8,128]{2,1,0:T(8,128)(2,1)S(1)}, bf16[16,8,128]{2,1,0:T(8,128)(2,1)S(1)}, u32[]{:S(2)}, u32[]{:S(2)}) collective-permute-start(bf16[16,8,128]{2,1,0:T(8,128)(2,1)S(1)} %get-tuple-element.9), channel_id=1, source_target_pairs={{1,0},{2,1},{3,2},{4,3},{5,4},{6,5},{7,6},{8,7},{9,8},{10,9},{11,1... | collective-permute-start | bytes 98312 | tf_op jit(solution)/shard_map/ppermute | solution.py:262
  38.7 0.0 copy-done.1
  38.7 0.0 copy-done.2
  38.7 0.1 copy.20
  38.8 0.1 reshape.23.pattern_ref
  38.9 0.0 collective-permute-done.below_ref
  38.9 3.1 %collective-permute-done.1.above_ref = bf16[16,8,128]{2,1,0:T(8,128)(2,1)S(1)} collective-permute-done((bf16[16,8,128]{2,1,0:T(8,128)(2,1)S(1)}, bf16[16,8,128]{2,1,0:T(8,128)(2,1)S(1)}, u32[]{:S(2)}, u32[]{:S(2)}) %collective-permute-start.1) | collective-permute-done | bytes 32800 | tf_op jit(solution)/shard_map/ppermute | solution.py:262
  42.0 0.1 shard_map.68
  42.1 3.7 %collective-permute-start.2 = (bf16[8,128,128]{2,1,0:T(8,128)(2,1)S(1)}, bf16[8,128,128]{2,1,0:T(8,128)(2,1)S(1)}, u32[]{:S(2)}, u32[]{:S(2)}) collective-permute-start(bf16[8,128,128]{2,1,0:T(8,128)(2,1)S(1)} %get-tuple-element.7.last_ref), channel_id=1, source_target_pairs={{0,16},{16,32},{32,48},{48,64},{64,80},{80,96},{96,112},{112,128},... | collective-permute-start | bytes 786440 | tf_op jit(solution)/shard_map/ppermute | solution.py:261
  45.7 1.3 %collective-permute-start.3 = (bf16[8,128,128]{2,1,0:T(8,128)(2,1)S(1)}, bf16[8,128,128]{2,1,0:T(8,128)(2,1)S(1)}, u32[]{:S(2)}, u32[]{:S(2)}) collective-permute-start(bf16[8,128,128]{2,1,0:T(8,128)(2,1)S(1)} %get-tuple-element.8.first_ref), channel_id=1, source_target_pairs={{16,0},{32,16},{48,32},{64,48},{80,64},{96,80},{112,96},{128,112},... | collective-permute-start | bytes 786440 | tf_op jit(solution)/shard_map/ppermute | solution.py:262
  47.0 0.1 all-to-all-done.1.got_ref
  47.1 0.9 %shard_map.66.after_ref = f32[128,128]{1,0:T(8,128)} custom-call(bf16[16,72,128]{2,1,0:T(8,128)(2,1)S(1)} %all-to-all-done.1.got_ref), custom_call_target="tpu_custom_call" | custom-call | flops 20000000000 | bytes 1000000 | tf_op jit(solution)/shard_map/pallas_call | solution.py:134
  48.1 10.3 %all-to-all-start.2 = ((f32[32,4,128]{2,1,0:T(4,128)}), f32[32,4,128]{2,1,0:T(4,128)S(1)}, u32[]{:S(2)}, u32[]{:S(2)}) async-start(f32[32,4,128]{2,1,0:T(4,128)} %bitcast.4), calls=%async_computation.2 | async-start | bytes 131072 | tf_op jit(solution)/shard_map/all_to_all | solution.py:288
  58.4 0.3 copy.19
  58.7 0.1 pad.4.basis_ref
  58.8 0.0 collective-permute-done.2.left_ref
  58.8 0.0 collective-permute-done.3.right_ref
  58.8 2.6 %shard_map.69.local_ref = f32[16,112,128]{2,1,0:T(8,128)S(1)} custom-call(s32[96]{0:T(128)S(1)} %reshape.23.pattern_ref, bf16[8,128,128]{2,1,0:T(8,128)(2,1)S(1)} %collective-permute-done.2.left_ref, bf16[8,128,128]{2,1,0:T(8,128)(2,1)S(1)} %get-tuple-element.8.first_ref, bf16[8,128,128]{2,1,0:T(8,128)(2,1)S(1)} %get-tuple-element.7.last_ref, ...), custom_call_target="tpu_custom_call" | custom-call | tf_op jit(solution)/shard_map/pallas_call | solution.py:208
  61.5 4.1 %all-to-all-done.2 = f32[32,4,128]{2,1,0:T(4,128)S(1)} async-done(((f32[32,4,128]{2,1,0:T(4,128)}), f32[32,4,128]{2,1,0:T(4,128)S(1)}, u32[]{:S(2)}, u32[]{:S(2)}) %all-to-all-start.2) | async-done | bytes 65568 | tf_op jit(solution)/shard_map/all_to_all | solution.py:288
  65.5 1.1 %shard_map.70 = f32[16,112,128]{2,1,0:T(8,128)} custom-call(f32[128,128]{1,0:T(8,128)S(1)} %bitcast.11, bf16[16,112,128]{2,1,0:T(8,128)(2,1)S(1)} %pad.4.basis_ref, f32[16,112,128]{2,1,0:T(8,128)S(1)} %shard_map.69.local_ref), custom_call_target="tpu_custom_call" | custom-call | tf_op jit(solution)/shard_map/pallas_call | solution.py:248
  (4 shorter events, 0.0 us)
Async XLA Ops:
  1.9 17.5 %all-to-all-start = ((bf16[32,4,128]{2,1,0:T(4,128)(2,1)}), bf16[32,4,128]{2,1,0:T(4,128)(2,1)S(1)}, u32[]{:S(2)}, u32[]{:S(2)}) async-start(bf16[32,4,128]{2,1,0:T(4,128)(2,1)} %bitcast.15), calls=%async_computation | async-start | bytes 65536 | tf_op jit(solution)/shard_map/all_to_all | solution.py:276
  19.4 14.1 %copy-start = (f32[16,112,128]{2,1,0:T(8,128)S(1)}, f32[16,112,128]{2,1,0:T(8,128)}, u32[]{:S(2)}) copy-start(f32[16,112,128]{2,1,0:T(8,128)} %cells_ref.1) | copy-start | bytes 2752516
  19.4 19.3 %copy-start.1 = (f32[4,16,112]{2,1,0:T(8,128)S(1)}, f32[4,16,112]{2,1,0:T(8,128)}, u32[]{:S(2)}) copy-start(f32[4,16,112]{2,1,0:T(8,128)} %param.7) | copy-start | bytes 86020
  19.4 19.3 %copy-start.2 = (s32[1,1,32,3]{2,1,3,0:T(1,128)S(1)}, s32[1,1,32,3]{2,1,3,0:T(1,128)}, u32[]{:S(2)}) copy-start(s32[1,1,32,3]{2,1,3,0:T(1,128)} %param.9) | copy-start | bytes 1156
  20.4 26.7 %all-to-all-start.1 = ((bf16[16,72,128]{2,1,0:T(8,128)(2,1)}), bf16[16,72,128]{2,1,0:T(8,128)(2,1)S(1)}, u32[]{:S(2)}, u32[]{:S(2)}) async-start(bf16[16,72,128]{2,1,0:T(8,128)(2,1)} %shard_map.65.after_ref), calls=%async_computation.1 | async-start | bytes 589824 | tf_op jit(solution)/shard_map/all_to_all | solution.py:287
  33.6 5.3 %collective-permute-start = (bf16[16,8,128]{2,1,0:T(8,128)(2,1)S(1)}, bf16[16,8,128]{2,1,0:T(8,128)(2,1)S(1)}, u32[]{:S(2)}, u32[]{:S(2)}) collective-permute-start(bf16[16,8,128]{2,1,0:T(8,128)(2,1)S(1)} %get-tuple-element.10), channel_id=1, source_target_pairs={{0,1},{1,2},{2,3},{3,4},{4,5},{5,6},{6,7},{7,8},{8,9},{9,10},{10,1... | collective-permute-start | bytes 98312 | tf_op jit(solution)/shard_map/ppermute | solution.py:261
  36.7 5.2 %collective-permute-start.1 = (bf16[16,8,128]{2,1,0:T(8,128)(2,1)S(1)}, bf16[16,8,128]{2,1,0:T(8,128)(2,1)S(1)}, u32[]{:S(2)}, u32[]{:S(2)}) collective-permute-start(bf16[16,8,128]{2,1,0:T(8,128)(2,1)S(1)} %get-tuple-element.9), channel_id=1, source_target_pairs={{1,0},{2,1},{3,2},{4,3},{5,4},{6,5},{7,6},{8,7},{9,8},{10,9},{11,1... | collective-permute-start | bytes 98312 | tf_op jit(solution)/shard_map/ppermute | solution.py:262
  42.1 16.7 %collective-permute-start.2 = (bf16[8,128,128]{2,1,0:T(8,128)(2,1)S(1)}, bf16[8,128,128]{2,1,0:T(8,128)(2,1)S(1)}, u32[]{:S(2)}, u32[]{:S(2)}) collective-permute-start(bf16[8,128,128]{2,1,0:T(8,128)(2,1)S(1)} %get-tuple-element.7.last_ref), channel_id=1, source_target_pairs={{0,16},{16,32},{32,48},{48,64},{64,80},{80,96},{96,112},{112,128},... | collective-permute-start | bytes 786440 | tf_op jit(solution)/shard_map/ppermute | solution.py:261
  45.7 13.1 %collective-permute-start.3 = (bf16[8,128,128]{2,1,0:T(8,128)(2,1)S(1)}, bf16[8,128,128]{2,1,0:T(8,128)(2,1)S(1)}, u32[]{:S(2)}, u32[]{:S(2)}) collective-permute-start(bf16[8,128,128]{2,1,0:T(8,128)(2,1)S(1)} %get-tuple-element.8.first_ref), channel_id=1, source_target_pairs={{16,0},{32,16},{48,32},{64,48},{80,64},{96,80},{112,96},{128,112},... | collective-permute-start | bytes 786440 | tf_op jit(solution)/shard_map/ppermute | solution.py:262
  48.1 17.4 %all-to-all-start.2 = ((f32[32,4,128]{2,1,0:T(4,128)}), f32[32,4,128]{2,1,0:T(4,128)S(1)}, u32[]{:S(2)}, u32[]{:S(2)}) async-start(f32[32,4,128]{2,1,0:T(4,128)} %bitcast.4), calls=%async_computation.2 | async-start | bytes 131072 | tf_op jit(solution)/shard_map/all_to_all | solution.py:288

commit v4 on v3

--- a/solution.py
+++ b/solution.py
@@ -83,24 +83,25 @@
     held = held_ref.shape[0]
     slots = place_ref.shape[1]
     ncl = contrib_ref.shape[0]
-    depth = out_ref.shape[1] - 2 * ncl
+    tile = 4 * ncl
+    depth = out_ref.shape[1] - tile
     turned = held_ref[...].astype(F32).T[:depth].astype(BF)
     rows = lax.broadcasted_iota(jnp.int32, (held, slots), 0)
     contrib = contrib_ref[...]
     coarse = contrib.astype(BF).astype(F32)
-    both = jnp.concatenate([coarse, contrib - coarse], axis=0).astype(BF)
+    both = jnp.concatenate([coarse, contrib - coarse, jnp.zeros((2 * ncl, slots), F32)], axis=0).astype(BF)
     for z in range(place_ref.shape[0]):
         pick = (rows == place_ref[z : z + 1, :]).astype(F32).astype(BF)
         sent = jnp.dot(turned, pick, preferred_element_type=F32)
         out_ref[z, 0:depth, :] = sent.astype(BF)
-        out_ref[z, depth : depth + 2 * ncl, :] = both
+        out_ref[z, depth : depth + tile, :] = both
 
 
 def route(held, place, contrib):
     nz, slots = place.shape
     return pl.pallas_call(
         route_kernel,
-        out_shape=jax.ShapeDtypeStruct((nz, (nz + 2) * contrib.shape[0], slots), BF),
+        out_shape=jax.ShapeDtypeStruct((nz, (nz + 4) * contrib.shape[0], slots), BF),
         in_specs=[VMEM, VMEM, VMEM],
         out_specs=VMEM,
         compiler_params=GRANT,
@@ -111,15 +112,15 @@
 def apply_kernel(got_ref, out_ref):
     nz, rows, lanes = got_ref.shape
     ncl = NCL
-    depth = rows - 2 * ncl
+    depth = rows - 4 * ncl
     block = got_ref[0, 0:depth, :].astype(F32)
     for z in range(1, nz):
         block += got_ref[z, 0:depth, :].astype(F32)
     upper = lax.broadcasted_iota(jnp.int32, (2 * ncl, lanes), 0) < ncl
     high, low = [], []
     for q in range(nz // 2):
-        one = got_ref[2 * q, depth:rows, :].astype(F32)
-        two = got_ref[2 * q + 1, depth:rows, :].astype(F32)
+        one = got_ref[2 * q, depth:rows, :].astype(F32)[: 2 * ncl]
+        two = got_ref[2 * q + 1, depth:rows, :].astype(F32)[: 2 * ncl]
         high.append(jnp.where(upper, one, pltpu.roll(two, ncl, 0)))
         low.append(jnp.where(upper, pltpu.roll(one, ncl, 0), two))
     turned = block.T.astype(BF)
@@ -161,11 +162,12 @@
     rows = first_ref.shape[0]
     for start, out_ref in ((0, first_ref), (rows, last_ref)):
         part = slice(start, start + rows)
-        out_ref[...] = jnp.concatenate([below_ref[part], mid_ref[part], above_ref[part]], axis=1)
+        below, above = below_ref[part][:, W:], above_ref[part][:, :W]
+        out_ref[...] = jnp.concatenate([below, mid_ref[part], above], axis=1)
 
 
 def widen(below, mid, above):
-    wide = below.shape[1] + mid.shape[1] + above.shape[1]
+    wide = mid.shape[1] + 2 * W
     shape = jax.ShapeDtypeStruct((mid.shape[0] // 2, wide, mid.shape[2]), BF)
     return pl.pallas_call(
         widen_kernel,
@@ -281,7 +283,7 @@
     sent = route(held, place, contrib)
 
     rounded = round_cells(residual, sent)
-    below, above = neighbours(rounded[:, own_y - W :], rounded[:, :W], "py")
+    below, above = neighbours(rounded[:, own_y - 2 * W :], rounded[:, : 2 * W], "py")
     first, last = widen(below, rounded, above)
     left, right = neighbours(last, first, ("z", "h"))
     partial = apply_block(lax.all_to_all(sent, "z", 0, 0))

time: 67.2 us -> 69.7 us (1.037)
  waiting for transfers between devices: 11.1 us -> 12.7 us
  starting transfers between devices: 43.7 us -> 44.6 us
    all_to_all x1, waiting for transfers between devices: 0.11 us -> 1.26 us  [body(): partial = apply_block(lax.all_to_all(sent, 'z', 0, 0))]
    all_to_all x1, starting transfers between devices: 10.3 us -> 11.3 us  [body(): lax.all_to_all(partial.reshape(plane, ncl, vectors), ('h', 'py'), 0, 0)]
  transfers between devices with their start and end apart: 7 -> 7, of which waited for: 4 -> 4; matrix products, arithmetic and copies ran while one was open for 6% -> 6% of each run, Pallas kernels for 6% -> 5%
where the time goes in v4:
time: 69.7 us; the launch traced here: 69.1 us
  starting transfers between devices  44.6 us (64%)
  waiting for transfers between devices  12.7 us (18%)
  Pallas kernels  7.84 us (11%)
  matrix products  2.08 us (3%)
  local copies, waits for them, and re-layouts  1.71 us (2%)
    all_to_all x1, starting transfers between devices, body(): partial = apply_block(lax.all_to_all(sent, 'z', 0, 0))  13 us
    all_to_all x1, starting transfers between devices, body(): lax.all_to_all(partial.reshape(plane, ncl, vectors), ('h', 'py'), 0, 0)  11.3 us
    all_to_all x1, starting transfers between devices, body(): held = lax.all_to_all(columns, ('h', 'py'), 0, 0).reshape(slots, 2 * depth)  10.4 us
    ppermute x2, starting transfers between devices, neighbours(): lax.ppermute(tail, axis, [(i, i + 1) for i in range(ends)])  6.76 us
    all_to_all x1, waiting for transfers between devices, body(): lax.all_to_all(partial.reshape(plane, ncl, vectors), ('h', 'py'), 0, 0)  4.06 us
    all_to_all x1, waiting for transfers between devices, body(): held = lax.all_to_all(columns, ('h', 'py'), 0, 0).reshape(slots, 2 * depth)  3.91 us
    ppermute x2, waiting for transfers between devices, neighbours(): lax.ppermute(head, axis, [(i + 1, i) for i in range(ends)])  3.42 us
    ppermute x2, starting transfers between devices, neighbours(): lax.ppermute(head, axis, [(i + 1, i) for i in range(ends)])  3.21 us
  transfers between devices with their start and end apart: 7, of which 4 were waited for; matrix products, arithmetic and copies ran while one was open for 6% of the time, Pallas kernels for 5%

profile of v4, /device:TPU:1, one launch (start us, length us, event | category | flops | bytes accessed | tf_op | source)
XLA Modules:
  0.0 69.1 jit_solution(14676788261758591939)
XLA Ops:
  0.0 1.9 %shard_map.64 = bf16[128,128]{1,0:T(8,128)(2,1)} custom-call(f32[4,2048]{1,0:T(4,128)} %rows_hbm.1, s32[16,4,32]{2,1,0:T(4,128)} %bitcast.14), custom_call_target="tpu_custom_call" | custom-call | tf_op jit(solution)/shard_map/pallas_call | solution.py:68
  1.9 10.4 %all-to-all-start = ((bf16[32,4,128]{2,1,0:T(4,128)(2,1)}), bf16[32,4,128]{2,1,0:T(4,128)(2,1)S(1)}, u32[]{:S(2)}, u32[]{:S(2)}) async-start(bf16[32,4,128]{2,1,0:T(4,128)(2,1)} %bitcast.15), calls=%async_computation | async-start | bytes 65536 | tf_op jit(solution)/shard_map/all_to_all | solution.py:278
  12.3 1.0 %copy.17 = s32[32,16,4]{2,1,0:T(8,128)S(1)} copy(s32[32,16,4]{0,2,1:T(4,128)} %param.10) | data formatting | bytes 16384 | tf_op args[4]
  13.2 0.2 reshape.20
  13.4 2.1 %convolution_bitcast_fusion.contrib_ref = f32[4,128]{1,0:T(4,128)S(1)} fusion(f32[16,112,128]{2,1,0:T(8,128)} %cells_ref.1, f32[4,16,112]{2,1,0:T(8,128)} %param.7), kind=kOutput, calls=%fused_computation | convolution fusion | flops 11010048 | bytes 948224 | tf_op jit(solution)/shard_map/lxy,xyr->lr/dot_general | solution.py:282
  15.5 3.9 %all-to-all-done = bf16[32,4,128]{2,1,0:T(4,128)(2,1)S(1)} async-done(((bf16[32,4,128]{2,1,0:T(4,128)(2,1)}), bf16[32,4,128]{2,1,0:T(4,128)(2,1)S(1)}, u32[]{:S(2)}, u32[]{:S(2)}) %all-to-all-start) | async-done | bytes 32800 | tf_op jit(solution)/shard_map/all_to_all | solution.py:278
  19.4 0.0 copy-start
  19.4 0.0 copy-start.1
  19.4 0.0 copy-start.2
  19.4 1.1 %shard_map.65.after_ref = bf16[16,80,128]{2,1,0:T(8,128)(2,1)} custom-call(bf16[128,128]{1,0:T(8,128)(2,1)S(1)} %bitcast.12, s32[16,128]{1,0:T(8,128)S(1)} %fusion.3.place_ref, f32[4,128]{1,0:T(4,128)S(1)} %convolution_bitcast_fusion.contrib_ref), custom_call_target="tpu_custom_call" | custom-call | flops 20000000000 | bytes 1000000 | tf_op jit(solution)/shard_map/pallas_call | solution.py:102
  20.5 13.0 %all-to-all-start.1 = ((bf16[16,80,128]{2,1,0:T(8,128)(2,1)}), bf16[16,80,128]{2,1,0:T(8,128)(2,1)S(1)}, u32[]{:S(2)}, u32[]{:S(2)}) async-start(bf16[16,80,128]{2,1,0:T(8,128)(2,1)} %shard_map.65.after_ref), calls=%async_computation.1 | async-start | bytes 655360 | tf_op jit(solution)/shard_map/all_to_all | solution.py:289
  33.5 0.0 copy-done
  33.5 0.1 shard_map.67.mid_ref
  33.6 3.1 %collective-permute-start = (bf16[16,16,128]{2,1,0:T(8,128)(2,1)S(1)}, bf16[16,16,128]{2,1,0:T(8,128)(2,1)S(1)}, u32[]{:S(2)}, u32[]{:S(2)}) collective-permute-start(bf16[16,16,128]{2,1,0:T(8,128)(2,1)S(1)} %get-tuple-element.10), channel_id=1, source_target_pairs={{0,1},{1,2},{2,3},{3,4},{4,5},{5,6},{6,7},{7,8},{8,9},{9,10},{10,1... | collective-permute-start | bytes 196616 | tf_op jit(solution)/shard_map/ppermute | solution.py:263
  36.7 1.9 %collective-permute-start.1 = (bf16[16,16,128]{2,1,0:T(8,128)(2,1)S(1)}, bf16[16,16,128]{2,1,0:T(8,128)(2,1)S(1)}, u32[]{:S(2)}, u32[]{:S(2)}) collective-permute-start(bf16[16,16,128]{2,1,0:T(8,128)(2,1)S(1)} %get-tuple-element.9), channel_id=1, source_target_pairs={{1,0},{2,1},{3,2},{4,3},{5,4},{6,5},{7,6},{8,7},{9,8},{10,9},{11,1... | collective-permute-start | bytes 196616 | tf_op jit(solution)/shard_map/ppermute | solution.py:264
  38.7 0.0 copy-done.1
  38.7 0.0 copy-done.2
  38.7 0.1 copy.20
  38.8 0.1 reshape.23.pattern_ref
  38.9 0.0 collective-permute-done.below_ref
  38.9 3.4 %collective-permute-done.1.above_ref = bf16[16,16,128]{2,1,0:T(8,128)(2,1)S(1)} collective-permute-done((bf16[16,16,128]{2,1,0:T(8,128)(2,1)S(1)}, bf16[16,16,128]{2,1,0:T(8,128)(2,1)S(1)}, u32[]{:S(2)}, u32[]{:S(2)}) %collective-permute-start.1) | collective-permute-done | bytes 65568 | tf_op jit(solution)/shard_map/ppermute | solution.py:264
  42.3 0.1 shard_map.68
  42.4 3.7 %collective-permute-start.2 = (bf16[8,128,128]{2,1,0:T(8,128)(2,1)S(1)}, bf16[8,128,128]{2,1,0:T(8,128)(2,1)S(1)}, u32[]{:S(2)}, u32[]{:S(2)}) collective-permute-start(bf16[8,128,128]{2,1,0:T(8,128)(2,1)S(1)} %get-tuple-element.7.last_ref), channel_id=1, source_target_pairs={{0,16},{16,32},{32,48},{48,64},{64,80},{80,96},{96,112},{112,128},... | collective-permute-start | bytes 786440 | tf_op jit(solution)/shard_map/ppermute | solution.py:263
  46.1 1.3 %collective-permute-start.3 = (bf16[8,128,128]{2,1,0:T(8,128)(2,1)S(1)}, bf16[8,128,128]{2,1,0:T(8,128)(2,1)S(1)}, u32[]{:S(2)}, u32[]{:S(2)}) collective-permute-start(bf16[8,128,128]{2,1,0:T(8,128)(2,1)S(1)} %get-tuple-element.8.first_ref), channel_id=1, source_target_pairs={{16,0},{32,16},{48,32},{64,48},{80,64},{96,80},{112,96},{128,112},... | collective-permute-start | bytes 786440 | tf_op jit(solution)/shard_map/ppermute | solution.py:264
  47.4 1.3 %all-to-all-done.1.got_ref = bf16[16,80,128]{2,1,0:T(8,128)(2,1)S(1)} async-done(((bf16[16,80,128]{2,1,0:T(8,128)(2,1)}), bf16[16,80,128]{2,1,0:T(8,128)(2,1)S(1)}, u32[]{:S(2)}, u32[]{:S(2)}) %all-to-all-start.1) | async-done | bytes 327712 | tf_op jit(solution)/shard_map/all_to_all | solution.py:289
  48.7 0.9 %shard_map.66.after_ref = f32[128,128]{1,0:T(8,128)} custom-call(bf16[16,80,128]{2,1,0:T(8,128)(2,1)S(1)} %all-to-all-done.1.got_ref), custom_call_target="tpu_custom_call" | custom-call | flops 20000000000 | bytes 1000000 | tf_op jit(solution)/shard_map/pallas_call | solution.py:135
  49.6 11.3 %all-to-all-start.2 = ((f32[32,4,128]{2,1,0:T(4,128)}), f32[32,4,128]{2,1,0:T(4,128)S(1)}, u32[]{:S(2)}, u32[]{:S(2)}) async-start(f32[32,4,128]{2,1,0:T(4,128)} %bitcast.4), calls=%async_computation.2 | async-start | bytes 131072 | tf_op jit(solution)/shard_map/all_to_all | solution.py:290
  60.9 0.3 copy.19
  61.2 0.1 pad.4.basis_ref
  61.3 0.0 collective-permute-done.2.left_ref
  61.3 0.0 collective-permute-done.3.right_ref
  61.3 2.6 %shard_map.69.local_ref = f32[16,112,128]{2,1,0:T(8,128)S(1)} custom-call(s32[96]{0:T(128)S(1)} %reshape.23.pattern_ref, bf16[8,128,128]{2,1,0:T(8,128)(2,1)S(1)} %collective-permute-done.2.left_ref, bf16[8,128,128]{2,1,0:T(8,128)(2,1)S(1)} %get-tuple-element.8.first_ref, bf16[8,128,128]{2,1,0:T(8,128)(2,1)S(1)} %get-tuple-element.7.last_ref, ...), custom_call_target="tpu_custom_call" | custom-call | tf_op jit(solution)/shard_map/pallas_call | solution.py:210
  63.9 4.1 %all-to-all-done.2 = f32[32,4,128]{2,1,0:T(4,128)S(1)} async-done(((f32[32,4,128]{2,1,0:T(4,128)}), f32[32,4,128]{2,1,0:T(4,128)S(1)}, u32[]{:S(2)}, u32[]{:S(2)}) %all-to-all-start.2) | async-done | bytes 65568 | tf_op jit(solution)/shard_map/all_to_all | solution.py:290
  68.0 1.1 %shard_map.70 = f32[16,112,128]{2,1,0:T(8,128)} custom-call(f32[128,128]{1,0:T(8,128)S(1)} %bitcast.11, bf16[16,112,128]{2,1,0:T(8,128)(2,1)S(1)} %pad.4.basis_ref, f32[16,112,128]{2,1,0:T(8,128)S(1)} %shard_map.69.local_ref), custom_call_target="tpu_custom_call" | custom-call | tf_op jit(solution)/shard_map/pallas_call | solution.py:250
  (4 shorter events, 0.0 us)
Async XLA Ops:
  1.9 17.5 %all-to-all-start = ((bf16[32,4,128]{2,1,0:T(4,128)(2,1)}), bf16[32,4,128]{2,1,0:T(4,128)(2,1)S(1)}, u32[]{:S(2)}, u32[]{:S(2)}) async-start(bf16[32,4,128]{2,1,0:T(4,128)(2,1)} %bitcast.15), calls=%async_computation | async-start | bytes 65536 | tf_op jit(solution)/shard_map/all_to_all | solution.py:278
  19.4 14.1 %copy-start = (f32[16,112,128]{2,1,0:T(8,128)S(1)}, f32[16,112,128]{2,1,0:T(8,128)}, u32[]{:S(2)}) copy-start(f32[16,112,128]{2,1,0:T(8,128)} %cells_ref.1) | copy-start | bytes 2752516
  19.4 19.3 %copy-start.1 = (f32[4,16,112]{2,1,0:T(8,128)S(1)}, f32[4,16,112]{2,1,0:T(8,128)}, u32[]{:S(2)}) copy-start(f32[4,16,112]{2,1,0:T(8,128)} %param.7) | copy-start | bytes 86020
  19.4 19.3 %copy-start.2 = (s32[1,1,32,3]{2,1,3,0:T(1,128)S(1)}, s32[1,1,32,3]{2,1,3,0:T(1,128)}, u32[]{:S(2)}) copy-start(s32[1,1,32,3]{2,1,3,0:T(1,128)} %param.9) | copy-start | bytes 1156
  20.5 28.2 %all-to-all-start.1 = ((bf16[16,80,128]{2,1,0:T(8,128)(2,1)}), bf16[16,80,128]{2,1,0:T(8,128)(2,1)S(1)}, u32[]{:S(2)}, u32[]{:S(2)}) async-start(bf16[16,80,128]{2,1,0:T(8,128)(2,1)} %shard_map.65.after_ref), calls=%async_computation.1 | async-start | bytes 655360 | tf_op jit(solution)/shard_map/all_to_all | solution.py:289
  33.6 5.3 %collective-permute-start = (bf16[16,16,128]{2,1,0:T(8,128)(2,1)S(1)}, bf16[16,16,128]{2,1,0:T(8,128)(2,1)S(1)}, u32[]{:S(2)}, u32[]{:S(2)}) collective-permute-start(bf16[16,16,128]{2,1,0:T(8,128)(2,1)S(1)} %get-tuple-element.10), channel_id=1, source_target_pairs={{0,1},{1,2},{2,3},{3,4},{4,5},{5,6},{6,7},{7,8},{8,9},{9,10},{10,1... | collective-permute-start | bytes 196616 | tf_op jit(solution)/shard_map/ppermute | solution.py:263
  36.7 5.6 %collective-permute-start.1 = (bf16[16,16,128]{2,1,0:T(8,128)(2,1)S(1)}, bf16[16,16,128]{2,1,0:T(8,128)(2,1)S(1)}, u32[]{:S(2)}, u32[]{:S(2)}) collective-permute-start(bf16[16,16,128]{2,1,0:T(8,128)(2,1)S(1)} %get-tuple-element.9), channel_id=1, source_target_pairs={{1,0},{2,1},{3,2},{4,3},{5,4},{6,5},{7,6},{8,7},{9,8},{10,9},{11,1... | collective-permute-start | bytes 196616 | tf_op jit(solution)/shard_map/ppermute | solution.py:264
  42.4 18.9 %collective-permute-start.2 = (bf16[8,128,128]{2,1,0:T(8,128)(2,1)S(1)}, bf16[8,128,128]{2,1,0:T(8,128)(2,1)S(1)}, u32[]{:S(2)}, u32[]{:S(2)}) collective-permute-start(bf16[8,128,128]{2,1,0:T(8,128)(2,1)S(1)} %get-tuple-element.7.last_ref), channel_id=1, source_target_pairs={{0,16},{16,32},{32,48},{48,64},{64,80},{80,96},{96,112},{112,128},... | collective-permute-start | bytes 786440 | tf_op jit(solution)/shard_map/ppermute | solution.py:263
  46.1 15.2 %collective-permute-start.3 = (bf16[8,128,128]{2,1,0:T(8,128)(2,1)S(1)}, bf16[8,128,128]{2,1,0:T(8,128)(2,1)S(1)}, u32[]{:S(2)}, u32[]{:S(2)}) collective-permute-start(bf16[8,128,128]{2,1,0:T(8,128)(2,1)S(1)} %get-tuple-element.8.first_ref), channel_id=1, source_target_pairs={{16,0},{32,16},{48,32},{64,48},{80,64},{96,80},{112,96},{128,112},... | collective-permute-start | bytes 786440 | tf_op jit(solution)/shard_map/ppermute | solution.py:264
  49.6 18.4 %all-to-all-start.2 = ((f32[32,4,128]{2,1,0:T(4,128)}), f32[32,4,128]{2,1,0:T(4,128)S(1)}, u32[]{:S(2)}, u32[]{:S(2)}) async-start(f32[32,4,128]{2,1,0:T(4,128)} %bitcast.4), calls=%async_computation.2 | async-start | bytes 131072 | tf_op jit(solution)/shard_map/all_to_all | solution.py:290

commit v5 on v3

--- a/solution.py
+++ b/solution.py
@@ -256,11 +256,12 @@
 
 
 def neighbours(tail, head, axis):
-    ends = lax.axis_size(axis) - 1
-    return (
-        lax.ppermute(tail, axis, [(i, i + 1) for i in range(ends)]),
-        lax.ppermute(head, axis, [(i + 1, i) for i in range(ends)]),
-    )
+    count = lax.axis_size(axis)
+    odd = lax.axis_index(axis) % 2 == 1
+    one = lax.ppermute(jnp.where(odd, head, tail), axis, [(i, i ^ 1) for i in range(count)])
+    inner = range(1, count - 1)
+    two = lax.ppermute(jnp.where(odd, tail, head), axis, [(i, ((i + 1) ^ 1) - 1) for i in inner])
+    return jnp.where(odd, one, two), jnp.where(odd, two, one)
 
 
 def body(residual, basis, inv_blocks, pattern, coarse_map, coarse_inv):

time: 67.2 us -> 67.2 us (level)
  starting transfers between devices: 43.7 us -> 42.2 us
  waiting for transfers between devices: 11.1 us -> 12.4 us
    ppermute x4, starting transfers between devices: 9.97 us -> 8.53 us  [the longest x2 5.76 us: neighbours(): lax.ppermute(jnp.where(odd, head, tail), axis, [(i, i ^ 1) for i in range...]
    all_to_all x1, waiting for transfers between devices: 0.11 us -> 1.49 us  [body(): partial = apply_block(lax.all_to_all(sent, 'z', 0, 0))]
where the time goes in v5:
time: 67.2 us; the launch traced here: 66.7 us
  starting transfers between devices  42.2 us (63%)
  waiting for transfers between devices  12.4 us (18%)
  Pallas kernels  7.83 us (12%)
  matrix products  2.08 us (3%)
  local copies, waits for them, and re-layouts  1.71 us (3%)
    all_to_all x1, starting transfers between devices, body(): partial = apply_block(lax.all_to_all(sent, 'z', 0, 0))  13 us
    all_to_all x1, starting transfers between devices, body(): held = lax.all_to_all(columns, ('h', 'py'), 0, 0).reshape(slots, 2 * depth)  10.4 us
    all_to_all x1, starting transfers between devices, body(): lax.all_to_all(partial.reshape(plane, ncl, vectors), ('h', 'py'), 0, 0)  10.3 us
    ppermute x2, starting transfers between devices, neighbours(): lax.ppermute(jnp.where(odd, head, tail), axis, [(i, i ^ 1) for i in range...  5.76 us
    all_to_all x1, waiting for transfers between devices, body(): lax.all_to_all(partial.reshape(plane, ncl, vectors), ('h', 'py'), 0, 0)  4.43 us
    all_to_all x1, waiting for transfers between devices, body(): held = lax.all_to_all(columns, ('h', 'py'), 0, 0).reshape(slots, 2 * depth)  3.9 us
    ppermute x2, starting transfers between devices, neighbours(): lax.ppermute(jnp.where(odd, tail, head), axis, [(i, (i + 1 ^ 1) - 1) for...  2.77 us
    pallas_call x1, Pallas kernels, solve(): pl.pallas_call(solve_kernel, in_specs=[pl.BlockSpec(memory_space=pltpu.SM...  2.63 us
  transfers between devices with their start and end apart: 7, of which 4 were waited for; matrix products, arithmetic and copies ran while one was open for 6% of the time, Pallas kernels for 6%

profile of v5, /device:TPU:1, one launch (start us, length us, event | category | flops | bytes accessed | tf_op | source)
XLA Modules:
  0.0 66.7 jit_solution(14915961739881307580)
XLA Ops:
  0.0 1.9 %shard_map.64 = bf16[128,128]{1,0:T(8,128)(2,1)} custom-call(f32[4,2048]{1,0:T(4,128)} %rows_hbm.1, s32[16,4,32]{2,1,0:T(4,128)} %bitcast.14), custom_call_target="tpu_custom_call" | custom-call | tf_op jit(solution)/shard_map/pallas_call | solution.py:68
  1.9 10.4 %all-to-all-start = ((bf16[32,4,128]{2,1,0:T(4,128)(2,1)}), bf16[32,4,128]{2,1,0:T(4,128)(2,1)S(1)}, u32[]{:S(2)}, u32[]{:S(2)}) async-start(bf16[32,4,128]{2,1,0:T(4,128)(2,1)} %bitcast.15), calls=%async_computation | async-start | bytes 65536 | tf_op jit(solution)/shard_map/all_to_all | solution.py:277
  12.3 1.0 %copy.17 = s32[32,16,4]{2,1,0:T(8,128)S(1)} copy(s32[32,16,4]{0,2,1:T(4,128)} %param.10) | data formatting | bytes 16384 | tf_op args[4]
  13.2 0.2 reshape.20
  13.4 2.1 %convolution_bitcast_fusion.contrib_ref = f32[4,128]{1,0:T(4,128)S(1)} fusion(f32[16,112,128]{2,1,0:T(8,128)} %cells_ref.1, f32[4,16,112]{2,1,0:T(8,128)} %param.7), kind=kOutput, calls=%fused_computation | convolution fusion | flops 11010048 | bytes 948224 | tf_op jit(solution)/shard_map/lxy,xyr->lr/dot_general | solution.py:281
  15.5 3.9 %all-to-all-done = bf16[32,4,128]{2,1,0:T(4,128)(2,1)S(1)} async-done(((bf16[32,4,128]{2,1,0:T(4,128)(2,1)}), bf16[32,4,128]{2,1,0:T(4,128)(2,1)S(1)}, u32[]{:S(2)}, u32[]{:S(2)}) %all-to-all-start) | async-done | bytes 32800 | tf_op jit(solution)/shard_map/all_to_all | solution.py:277
  19.4 0.0 copy-start.1
  19.4 0.0 copy-start
  19.4 0.0 copy-start.2
  19.4 1.0 %shard_map.65.after_ref = bf16[16,72,128]{2,1,0:T(8,128)(2,1)} custom-call(bf16[128,128]{1,0:T(8,128)(2,1)S(1)} %bitcast.12, s32[16,128]{1,0:T(8,128)S(1)} %fusion.3.place_ref, f32[4,128]{1,0:T(4,128)S(1)} %convolution_bitcast_fusion.contrib_ref), custom_call_target="tpu_custom_call" | custom-call | flops 20000000000 | bytes 1000000 | tf_op jit(solution)/shard_map/pallas_call | solution.py:101
  20.4 13.0 %all-to-all-start.1 = ((bf16[16,72,128]{2,1,0:T(8,128)(2,1)}), bf16[16,72,128]{2,1,0:T(8,128)(2,1)S(1)}, u32[]{:S(2)}, u32[]{:S(2)}) async-start(bf16[16,72,128]{2,1,0:T(8,128)(2,1)} %shard_map.65.after_ref), calls=%async_computation.1 | async-start | bytes 589824 | tf_op jit(solution)/shard_map/all_to_all | solution.py:288
  33.5 0.0 copy-done.1
  33.5 0.0 copy-done
  33.5 0.1 shard_map.67.mid_ref
  33.7 2.9 %collective-permute-start = (bf16[16,8,128]{2,1,0:T(8,128)(2,1)S(1)}, bf16[16,8,128]{2,1,0:T(8,128)(2,1)S(1)}, u32[]{:S(2)}, u32[]{:S(2)}) collective-permute-start(bf16[16,8,128]{2,1,0:T(8,128)(2,1)S(1)} %get-tuple-element.14), channel_id=1, source_target_pairs={{0,1},{1,0},{2,3},{3,2},{4,5},{5,4},{6,7},{7,6},{8,9},{9,8},{10,11... | collective-permute-start | bytes 98312 | tf_op jit(solution)/shard_map/ppermute | solution.py:261
  36.6 2.1 %collective-permute-start.1 = (bf16[16,8,128]{2,1,0:T(8,128)(2,1)S(1)}, bf16[16,8,128]{2,1,0:T(8,128)(2,1)S(1)}, u32[]{:S(2)}, u32[]{:S(2)}) collective-permute-start(bf16[16,8,128]{2,1,0:T(8,128)(2,1)S(1)} %get-tuple-element.13), channel_id=1, source_target_pairs={{1,2},{2,1},{3,4},{4,3},{5,6},{6,5},{7,8},{8,7},{9,10},{10,9},{11,... | collective-permute-start | bytes 98312 | tf_op jit(solution)/shard_map/ppermute | solution.py:263
  38.7 0.0 copy-done.2
  38.8 0.1 copy.20
  38.8 0.1 reshape.23.pattern_ref
  38.9 0.3 copy.19
  39.2 0.1 pad.4.basis_ref
  39.3 0.0 collective-permute-done
  39.4 2.6 %collective-permute-done.1 = bf16[16,8,128]{2,1,0:T(8,128)(2,1)S(1)} collective-permute-done((bf16[16,8,128]{2,1,0:T(8,128)(2,1)S(1)}, bf16[16,8,128]{2,1,0:T(8,128)(2,1)S(1)}, u32[]{:S(2)}, u32[]{:S(2)}) %collective-permute-start.1) | collective-permute-done | bytes 32800 | tf_op jit(solution)/shard_map/ppermute | solution.py:263
  42.0 0.1 shard_map.68
  42.1 2.8 %collective-permute-start.2 = (bf16[8,128,128]{2,1,0:T(8,128)(2,1)S(1)}, bf16[8,128,128]{2,1,0:T(8,128)(2,1)S(1)}, u32[]{:S(2)}, u32[]{:S(2)}) collective-permute-start(bf16[8,128,128]{2,1,0:T(8,128)(2,1)S(1)} %get-tuple-element.12), channel_id=1, source_target_pairs={{0,16},{16,0},{32,48},{48,32},{64,80},{80,64},{96,112},{112,96},{1... | collective-permute-start | bytes 786440 | tf_op jit(solution)/shard_map/ppermute | solution.py:261
  45.0 0.7 %collective-permute-start.3 = (bf16[8,128,128]{2,1,0:T(8,128)(2,1)S(1)}, bf16[8,128,128]{2,1,0:T(8,128)(2,1)S(1)}, u32[]{:S(2)}, u32[]{:S(2)}) collective-permute-start(bf16[8,128,128]{2,1,0:T(8,128)(2,1)S(1)} %get-tuple-element.11), channel_id=1, source_target_pairs={{16,32},{32,16},{48,64},{64,48},{80,96},{96,80},{112,128},{128,112... | collective-permute-start | bytes 786440 | tf_op jit(solution)/shard_map/ppermute | solution.py:263
  45.6 1.5 %all-to-all-done.1.got_ref = bf16[16,72,128]{2,1,0:T(8,128)(2,1)S(1)} async-done(((bf16[16,72,128]{2,1,0:T(8,128)(2,1)}), bf16[16,72,128]{2,1,0:T(8,128)(2,1)S(1)}, u32[]{:S(2)}, u32[]{:S(2)}) %all-to-all-start.1) | async-done | bytes 294944 | tf_op jit(solution)/shard_map/all_to_all | solution.py:288
  47.1 0.9 %shard_map.66.after_ref = f32[128,128]{1,0:T(8,128)} custom-call(bf16[16,72,128]{2,1,0:T(8,128)(2,1)S(1)} %all-to-all-done.1.got_ref), custom_call_target="tpu_custom_call" | custom-call | flops 20000000000 | bytes 1000000 | tf_op jit(solution)/shard_map/pallas_call | solution.py:134
  48.1 10.3 %all-to-all-start.2 = ((f32[32,4,128]{2,1,0:T(4,128)}), f32[32,4,128]{2,1,0:T(4,128)S(1)}, u32[]{:S(2)}, u32[]{:S(2)}) async-start(f32[32,4,128]{2,1,0:T(4,128)} %bitcast.4), calls=%async_computation.2 | async-start | bytes 131072 | tf_op jit(solution)/shard_map/all_to_all | solution.py:289
  58.4 0.0 collective-permute-done.2
  58.4 0.0 collective-permute-done.3
  58.4 2.6 %shard_map.69.local_ref = f32[16,112,128]{2,1,0:T(8,128)S(1)} custom-call(s32[96]{0:T(128)S(1)} %reshape.23.pattern_ref, bf16[8,128,128]{2,1,0:T(8,128)(2,1)S(1)} %get-tuple-element.10.left_ref, bf16[8,128,128]{2,1,0:T(8,128)(2,1)S(1)} %get-tuple-element.7.first_ref, bf16[8,128,128]{2,1,0:T(8,128)(2,1)S(1)} %get-tuple-element.8.last_ref, ...), custom_call_target="tpu_custom_call" | custom-call | tf_op jit(solution)/shard_map/pallas_call | solution.py:208
  61.1 4.4 %all-to-all-done.2 = f32[32,4,128]{2,1,0:T(4,128)S(1)} async-done(((f32[32,4,128]{2,1,0:T(4,128)}), f32[32,4,128]{2,1,0:T(4,128)S(1)}, u32[]{:S(2)}, u32[]{:S(2)}) %all-to-all-start.2) | async-done | bytes 65568 | tf_op jit(solution)/shard_map/all_to_all | solution.py:289
  65.5 1.1 %shard_map.70 = f32[16,112,128]{2,1,0:T(8,128)} custom-call(f32[128,128]{1,0:T(8,128)S(1)} %bitcast.11, bf16[16,112,128]{2,1,0:T(8,128)(2,1)S(1)} %pad.4.basis_ref, f32[16,112,128]{2,1,0:T(8,128)S(1)} %shard_map.69.local_ref), custom_call_target="tpu_custom_call" | custom-call | tf_op jit(solution)/shard_map/pallas_call | solution.py:248
  (7 shorter events, 0.1 us)
Async XLA Ops:
  1.9 17.5 %all-to-all-start = ((bf16[32,4,128]{2,1,0:T(4,128)(2,1)}), bf16[32,4,128]{2,1,0:T(4,128)(2,1)S(1)}, u32[]{:S(2)}, u32[]{:S(2)}) async-start(bf16[32,4,128]{2,1,0:T(4,128)(2,1)} %bitcast.15), calls=%async_computation | async-start | bytes 65536 | tf_op jit(solution)/shard_map/all_to_all | solution.py:277
  19.4 14.1 %copy-start.1 = (f32[4,16,112]{2,1,0:T(8,128)S(1)}, f32[4,16,112]{2,1,0:T(8,128)}, u32[]{:S(2)}) copy-start(f32[4,16,112]{2,1,0:T(8,128)} %param.7) | copy-start | bytes 86020
  19.4 14.1 %copy-start = (f32[16,112,128]{2,1,0:T(8,128)S(1)}, f32[16,112,128]{2,1,0:T(8,128)}, u32[]{:S(2)}) copy-start(f32[16,112,128]{2,1,0:T(8,128)} %cells_ref.1) | copy-start | bytes 2752516
  19.4 19.3 %copy-start.2 = (s32[1,1,32,3]{2,1,3,0:T(1,128)S(1)}, s32[1,1,32,3]{2,1,3,0:T(1,128)}, u32[]{:S(2)}) copy-start(s32[1,1,32,3]{2,1,3,0:T(1,128)} %param.9) | copy-start | bytes 1156
  20.4 26.7 %all-to-all-start.1 = ((bf16[16,72,128]{2,1,0:T(8,128)(2,1)}), bf16[16,72,128]{2,1,0:T(8,128)(2,1)S(1)}, u32[]{:S(2)}, u32[]{:S(2)}) async-start(bf16[16,72,128]{2,1,0:T(8,128)(2,1)} %shard_map.65.after_ref), calls=%async_computation.1 | async-start | bytes 589824 | tf_op jit(solution)/shard_map/all_to_all | solution.py:288
  33.7 5.7 %collective-permute-start = (bf16[16,8,128]{2,1,0:T(8,128)(2,1)S(1)}, bf16[16,8,128]{2,1,0:T(8,128)(2,1)S(1)}, u32[]{:S(2)}, u32[]{:S(2)}) collective-permute-start(bf16[16,8,128]{2,1,0:T(8,128)(2,1)S(1)} %get-tuple-element.14), channel_id=1, source_target_pairs={{0,1},{1,0},{2,3},{3,2},{4,5},{5,4},{6,7},{7,6},{8,9},{9,8},{10,11... | collective-permute-start | bytes 98312 | tf_op jit(solution)/shard_map/ppermute | solution.py:261
  36.6 5.4 %collective-permute-start.1 = (bf16[16,8,128]{2,1,0:T(8,128)(2,1)S(1)}, bf16[16,8,128]{2,1,0:T(8,128)(2,1)S(1)}, u32[]{:S(2)}, u32[]{:S(2)}) collective-permute-start(bf16[16,8,128]{2,1,0:T(8,128)(2,1)S(1)} %get-tuple-element.13), channel_id=1, source_target_pairs={{1,2},{2,1},{3,4},{4,3},{5,6},{6,5},{7,8},{8,7},{9,10},{10,9},{11,... | collective-permute-start | bytes 98312 | tf_op jit(solution)/shard_map/ppermute | solution.py:263
  42.1 16.3 %collective-permute-start.2 = (bf16[8,128,128]{2,1,0:T(8,128)(2,1)S(1)}, bf16[8,128,128]{2,1,0:T(8,128)(2,1)S(1)}, u32[]{:S(2)}, u32[]{:S(2)}) collective-permute-start(bf16[8,128,128]{2,1,0:T(8,128)(2,1)S(1)} %get-tuple-element.12), channel_id=1, source_target_pairs={{0,16},{16,0},{32,48},{48,32},{64,80},{80,64},{96,112},{112,96},{1... | collective-permute-start | bytes 786440 | tf_op jit(solution)/shard_map/ppermute | solution.py:261
  45.0 13.4 %collective-permute-start.3 = (bf16[8,128,128]{2,1,0:T(8,128)(2,1)S(1)}, bf16[8,128,128]{2,1,0:T(8,128)(2,1)S(1)}, u32[]{:S(2)}, u32[]{:S(2)}) collective-permute-start(bf16[8,128,128]{2,1,0:T(8,128)(2,1)S(1)} %get-tuple-element.11), channel_id=1, source_target_pairs={{16,32},{32,16},{48,64},{64,48},{80,96},{96,80},{112,128},{128,112... | collective-permute-start | bytes 786440 | tf_op jit(solution)/shard_map/ppermute | solution.py:263
  48.1 17.4 %all-to-all-start.2 = ((f32[32,4,128]{2,1,0:T(4,128)}), f32[32,4,128]{2,1,0:T(4,128)S(1)}, u32[]{:S(2)}, u32[]{:S(2)}) async-start(f32[32,4,128]{2,1,0:T(4,128)} %bitcast.4), calls=%async_computation.2 | async-start | bytes 131072 | tf_op jit(solution)/shard_map/all_to_all | solution.py:289
